TPU v7x, 32 devices: a whole 2x2x4 slice. The times are simulated.
32 devices in a mesh: groups: 2 (over x), tiles: 8 (over z, y), sub: 2 (over core).
Axes of the slice: x: 2, y: 2, z: 4, core: 2. Of those that a mesh axis runs over, the one named last changes fastest.
Arguments:
- density: float32 [768, 1536], P(('groups', 'tiles'), 'sub'), parts along dimension 0, may hold values from 0.8 to 1.2
- momentum: float32 [3, 768, 1536], P(None, ('groups', 'tiles'), 'sub'), parts along dimension 1, may hold values from -0.4 to 0.4
- stress: float32 [6, 768, 1536], P(None, ('groups', 'tiles'), 'sub'), parts along dimension 1, may hold values from -0.4 to 0.4
- red_density: float32 [768, 1536], P(('groups', 'tiles'), 'sub'), parts along dimension 0, may hold values from 0.1 to 0.8
- solid: int32 [768, 1536], P(('groups', 'tiles'), 'sub'), parts along dimension 0, may hold values 0 or 1
- widths: int32 [16], P('groups'), parts along dimension 0, may hold values from 1 to 3, 16 in all
Outputs:
- density_next: float32 [768, 1536], P(('groups', 'tiles'), 'sub'), parts along dimension 0
- momentum_next: float32 [3, 768, 1536], P(None, ('groups', 'tiles'), 'sub'), parts along dimension 1
- stress_next: float32 [6, 768, 1536], P(None, ('groups', 'tiles'), 'sub'), parts along dimension 1
- red_next: float32 [768, 1536], P(('groups', 'tiles'), 'sub'), parts along dimension 0
There are 2 independent parts, one for each index of `groups`. A program takes and returns all parts, laid end to end along the dimension named above; each array names one. Nothing has to cross between parts.
Inputs may be any that keep to these rules, and one draw needn't show every extreme that they name: Device k along tiles owns the tile columns from widths[0] + ... + widths[k-1] on, widths[k] of them, alike in every part of sub; they sum to 16, and one equals 3. 1 marks a solid cell, 0 a pore cell.
All inputs are finite; a program needn't handle non-finite values. No bound on the sum of `solid` on one device may be relied on, other than what follows from the above.
Results may differ from a plain program's by a relative error of at most 0.0003.
Values sent between devices are 32-bit elements; how exact they have to be, the bound alone decides.
No kernel may reach another device: no remote copies, remote signals or barrier semaphores. Data moves between devices by JAX's collectives and lax.ppermute only.
A program may use at most 64 MiB of HBM per device.

v0:
```python
import jax
import jax.numpy as jnp
from jax import lax
from jax.sharding import PartitionSpec as P

TILE = 16
STEPS = 2


RELAX_TIME = 0.8
SURFACE = 0.1
SEPARATION = 0.7
VELOCITIES = (
    (0, 0, 0),
    (1, 0, 0),
    (-1, 0, 0),
    (0, 1, 0),
    (0, -1, 0),
    (0, 0, 1),
    (0, 0, -1),
    (1, 1, 0),
    (-1, -1, 0),
    (1, -1, 0),
    (-1, 1, 0),
    (1, 0, 1),
    (-1, 0, -1),
    (1, 0, -1),
    (-1, 0, 1),
    (0, 1, 1),
    (0, -1, -1),
    (0, 1, -1),
    (0, -1, 1),
)
WEIGHTS = (1.0 / 3.0,) + (1.0 / 18.0,) * 6 + (1.0 / 36.0,) * 12
OPPOSITE = (0, 2, 1, 4, 3, 6, 5, 8, 7, 10, 9, 12, 11, 14, 13, 16, 15, 18, 17)


def padded_2(cells, sides, width):
    for axis, dim in sides:
        count = lax.axis_size(axis)
        ends = count - 1
        head = lax.slice_in_dim(cells, 0, width, axis=dim)
        tail = lax.slice_in_dim(cells, cells.shape[dim] - width, cells.shape[dim], axis=dim)
        cells = jnp.concatenate(
            [
                lax.ppermute(tail, axis, [(i, (i + 1) % count) for i in range(ends)]),
                cells,
                lax.ppermute(head, axis, [((i + 1) % count, i) for i in range(ends)]),
            ],
            axis=dim,
        )
    return cells


def rebuild_row(velocity):
    vel_x, vel_y, vel_z = velocity
    one_third = 1.0 / 3.0
    return (
        1.0,
        3.0 * vel_x,
        3.0 * vel_y,
        3.0 * vel_z,
        4.5 * (vel_x * vel_x - one_third),
        4.5 * (vel_y * vel_y - one_third),
        4.5 * (vel_z * vel_z - one_third),
        9.0 * vel_x * vel_y,
        9.0 * vel_x * vel_z,
        9.0 * vel_y * vel_z,
    )


def project_row(velocity):
    vel_x, vel_y, vel_z = velocity
    one_third = 1.0 / 3.0
    return (
        1.0,
        1.0 * vel_x,
        1.0 * vel_y,
        1.0 * vel_z,
        vel_x * vel_x - one_third,
        vel_y * vel_y - one_third,
        vel_z * vel_z - one_third,
        1.0 * vel_x * vel_y,
        1.0 * vel_x * vel_z,
        1.0 * vel_y * vel_z,
    )


def combine(factors, operands):
    summed = None
    for factor, operand in zip(factors, operands):
        if factor != 0.0:
            product = factor * operand
            summed = product if summed is None else summed + product
    return summed


def population(direction, moments):
    return WEIGHTS[direction] * combine(rebuild_row(VELOCITIES[direction]), moments[:10])


def red_population(direction, moments):
    vel_x, vel_y, vel_z = VELOCITIES[direction]
    return WEIGHTS[direction] * combine(
        (1.0, 3.0 * vel_x, 3.0 * vel_y, 3.0 * vel_z), moments[10:14]
    )


def collide(fields, fluid_cells, gradient):
    density, flux_x, flux_y, flux_z = (fields[0], fields[1], fields[2], fields[3])
    stress = fields[4:10]
    red_density = fields[10]
    grad_x, grad_y, grad_z = gradient
    square = grad_x * grad_x + grad_y * grad_y + grad_z * grad_z
    inverse = lax.rsqrt(1.0 + square)
    strength = SURFACE * inverse
    trace_part = square / 3.0
    surface = (
        grad_x * grad_x - trace_part,
        grad_y * grad_y - trace_part,
        grad_z * grad_z - trace_part,
        grad_x * grad_y,
        grad_x * grad_z,
        grad_y * grad_z,
    )
    relaxing = 1.0 - 1.0 / RELAX_TIME
    post_stress = [
        jnp.where(fluid_cells, relaxing * before + strength * addend, before)
        for before, addend in zip(stress, surface)
    ]
    post_x = jnp.where(fluid_cells, flux_x, -flux_x)
    post_y = jnp.where(fluid_cells, flux_y, -flux_y)
    post_z = jnp.where(fluid_cells, flux_z, -flux_z)
    mixing = SEPARATION * red_density * (density - red_density) * inverse
    charge_x = jnp.where(fluid_cells, 0.5 * flux_x + mixing * grad_x, -0.5 * flux_x)
    charge_y = jnp.where(fluid_cells, 0.5 * flux_y + mixing * grad_y, -0.5 * flux_y)
    charge_z = jnp.where(fluid_cells, 0.5 * flux_z + mixing * grad_z, -0.5 * flux_z)
    second = [
        post_x * post_x + post_stress[0],
        post_y * post_y + post_stress[1],
        post_z * post_z + post_stress[2],
        post_x * post_y + post_stress[3],
        post_x * post_z + post_stress[4],
        post_y * post_z + post_stress[5],
    ]
    return [density, post_x, post_y, post_z] + second + [red_density, charge_x, charge_y, charge_z]


def accumulate(totals, direction, arrived, red_arrived):
    updated = []
    for position, factor in enumerate(project_row(VELOCITIES[direction])):
        if factor != 0.0:
            contribution = factor * arrived
            updated.append(
                contribution if totals[position] is None else totals[position] + contribution
            )
        else:
            updated.append(totals[position])
    updated.append(red_arrived if totals[10] is None else totals[10] + red_arrived)
    return updated


def finish(totals):
    flux_x, flux_y, flux_z = (totals[1], totals[2], totals[3])
    return [
        totals[0],
        flux_x,
        flux_y,
        flux_z,
        totals[4] - flux_x * flux_x,
        totals[5] - flux_y * flux_y,
        totals[6] - flux_z * flux_z,
        totals[7] - flux_x * flux_y,
        totals[8] - flux_x * flux_z,
        totals[9] - flux_y * flux_z,
        totals[10],
    ]


def pad_flat(array):
    return jnp.pad(array, ((0, 0), (0, 0), (1, 1)))


def shifted(padded, offset, step, row_count, flat_count):
    start_row = offset + step[0]
    start_col = 1 + (offset + step[1]) * TILE + step[2]
    return padded[:, start_row : start_row + row_count, start_col : start_col + flat_count]


def inside(geometry, margin, row_count, flat_count, step):
    first_dev, last_dev, low_sub, high_sub, live_rows, width_cells = geometry
    row_ids = lax.iota(jnp.int32, row_count) - margin + step[0]
    flat_ids = lax.iota(jnp.int32, flat_count)
    lane_ids = flat_ids // TILE - margin + step[1]
    depth_ids = flat_ids % TILE + step[2]
    outside_x = first_dev & (row_ids < 0) | last_dev & (row_ids >= live_rows)
    outside_yz = (
        low_sub & (lane_ids < 0)
        | high_sub & (lane_ids >= width_cells)
        | (depth_ids < 0)
        | (depth_ids >= TILE)
    )
    return jnp.logical_not(outside_x)[:, None] & jnp.logical_not(outside_yz)[None, :]


def edge_rows(local_rows, margin, live_rows):
    return jnp.concatenate(
        [
            local_rows[:, :margin],
            lax.dynamic_slice_in_dim(local_rows, live_rows - margin, margin, axis=1),
        ],
        axis=1,
    )


def widen_rows(local_rows, received, margin, live_rows):
    zero_rows = jnp.zeros((local_rows.shape[0], margin, local_rows.shape[2]), local_rows.dtype)
    extended = jnp.concatenate([received[:, :margin], local_rows, zero_rows], axis=1)
    return lax.dynamic_update_slice_in_dim(
        extended, received[:, 3 * margin :], margin + live_rows, axis=1
    )


def edge_lanes(widened, columns):
    return jnp.concatenate([widened[:, :, :columns], widened[:, :, -columns:]], axis=2)


def attach_lanes(widened, received, columns):
    return pad_flat(
        jnp.concatenate([received[:, :, :columns], widened, received[:, :, -columns:]], axis=2)
    )


def phase_rim(colour, live_rows):
    received = padded_2(edge_rows(colour, 1, live_rows), (("tiles", 1),), 1)
    widened = widen_rows(colour, received, 1, live_rows)
    lanes = padded_2(edge_lanes(widened, TILE), (("sub", 2),), TILE)
    return attach_lanes(widened, lanes, TILE)


def state_rim(post, live_rows):
    received = padded_2(edge_rows(post, 1, live_rows), (("tiles", 1),), 1)
    widened = widen_rows(post, received, 1, live_rows)
    lanes = padded_2(edge_lanes(widened, TILE), (("sub", 2),), TILE)
    return attach_lanes(widened, lanes, TILE)


def gradient_of(colour_pad, offset, margin, row_count, flat_count, geometry):
    centre = shifted(colour_pad, offset, (0, 0, 0), row_count, flat_count)[0]
    gradient = [jnp.zeros_like(centre) for component in range(3)]
    for direction in range(1, 19):
        velocity = VELOCITIES[direction]
        rolled = shifted(colour_pad, offset, velocity, row_count, flat_count)[0]
        neighbour = jnp.where(
            inside(geometry, margin, row_count, flat_count, velocity), rolled, centre
        )
        for component in range(3):
            if velocity[component] != 0:
                gradient[component] = (
                    gradient[component] + 3.0 * WEIGHTS[direction] * velocity[component] * neighbour
                )
    return gradient


def propagate(post_pad, geometry, row_count, flat_count):
    resident = shifted(post_pad, 1, (0, 0, 0), row_count, flat_count)
    resident_list = [resident[channel] for channel in range(14)]
    totals = [None] * 11
    for direction in range(19):
        velocity = VELOCITIES[direction]
        against = (-velocity[0], -velocity[1], -velocity[2])
        inward = inside(geometry, 0, row_count, flat_count, against)
        source = shifted(post_pad, 1, against, row_count, flat_count)
        source_list = [source[channel] for channel in range(14)]
        reverse = OPPOSITE[direction]
        arrived = jnp.where(
            inward, population(direction, source_list), population(reverse, resident_list)
        )
        red_arrived = jnp.where(
            inward, red_population(direction, source_list), red_population(reverse, resident_list)
        )
        totals = accumulate(totals, direction, arrived, red_arrived)
    return finish(totals)


def shallow_step(fields, fluid_cells, geometry, row_count, flat_count):
    live_rows = geometry[4]
    colour = (2.0 * fields[10] - fields[0])[None]
    colour_pad = phase_rim(colour, live_rows)
    gradient = gradient_of(colour_pad, 1, 0, row_count, flat_count, geometry)
    post = collide(fields, fluid_cells, gradient)
    post_pad = state_rim(jnp.stack(post), live_rows)
    return propagate(post_pad, geometry, row_count, flat_count)


def body(density, momentum, stress, red_density, solid, widths):
    row_count = density.shape[0]
    flat_count = density.shape[1]
    tiles_index = lax.axis_index("tiles")
    sub_index = lax.axis_index("sub")
    chosen = lax.iota(jnp.int32, widths.shape[0]) == tiles_index
    live_rows = jnp.sum(jnp.where(chosen, widths, 0)) * TILE
    geometry = (
        tiles_index == 0,
        tiles_index == lax.axis_size("tiles") - 1,
        sub_index == 0,
        sub_index == lax.axis_size("sub") - 1,
        live_rows,
        flat_count // TILE,
    )
    fields = [density] + [momentum[component] for component in range(3)]
    fields = fields + [stress[component] for component in range(6)] + [red_density]
    fluid_cells = solid == 0
    for repeat in range(STEPS):
        fields = shallow_step(fields, fluid_cells, geometry, row_count, flat_count)
    row_live = (lax.iota(jnp.int32, row_count) < live_rows)[:, None]
    results = [jnp.where(row_live, grid, 0.0) for grid in fields]
    return (results[0], jnp.stack(results[1:4]), jnp.stack(results[4:10]), results[10])


def solution(mesh):
    in_specs = (
        P(("groups", "tiles"), "sub"),
        P(None, ("groups", "tiles"), "sub"),
        P(None, ("groups", "tiles"), "sub"),
        P(("groups", "tiles"), "sub"),
        P(("groups", "tiles"), "sub"),
        P("groups"),
    )
    out_specs = (
        P(("groups", "tiles"), "sub"),
        P(None, ("groups", "tiles"), "sub"),
        P(None, ("groups", "tiles"), "sub"),
        P(("groups", "tiles"), "sub"),
    )
    return jax.shard_map(body, mesh=mesh, in_specs=in_specs, out_specs=out_specs, check_vma=False)
```

profile of v0, /device:TPU:0, one launch (start us, length us, event | category | flops | bytes accessed | tf_op | source)
XLA Modules:
  0.0 121.3 jit_solution(4091358884921264168)
XLA Ops:
  0.7 1.4 %fusion.827 = s32[]{:T(128)} fusion(s32[8]{0:T(128)} %param.11, s32[]{:T(128)S(6)} %axis_index.23), kind=kLoop, calls=%fused_computation.1938 | loop fusion | flops 23 | bytes 40 | tf_op jit(solution)/shard_map/reduce_sum | solution.py:302
  3.7 4.9 %collective-permute-start = (f32[1,1,768]{2,1,0:T(1,128)S(1)}, f32[1,1,768]{2,1,0:T(1,128)S(1)}, u32[]{:S(2)}, u32[]{:S(2)}) collective-permute-start(f32[1,1,768]{2,1,0:T(1,128)S(1)} %dynamic-slice_bitcast_fusion), channel_id=1, source_target_pairs={{0,2},{2,4},{4,6},{6,8},{8,10},{10,12},{12,14},{1,3},{3,5},{5,7},{... | collective-permute-start | bytes 9224 | tf_op jit(solution)/shard_map/ppermute | solution.py:46
  9.9 1.6 %bitcast_dynamic-update-slice_fusion.25 = f32[14,48,768]{2,1,0:T(8,128)} fusion(f32[48,768]{1,0:T(8,128)} %param.6), kind=kLoop, calls=%fused_computation.1762 | loop fusion | bytes 294912
  11.6 1.7 %bitcast_dynamic-update-slice_fusion.24 = (f32[14,48,768]{2,1,0:T(8,128)}, pred[48,768]{1,0:T(8,128)(4,1)S(1)}) fusion(f32[14,48,768]{2,1,0:T(8,128)} %bitcast_dynamic-update-slice_fusion.25, f32[3,48,768]{2,1,0:T(8,128)} %param.7, s32[48,768]{1,0:T(8,128)} %param.10), kind=kLoop, calls=%fused_computation.1757 | loop fusion | flops 110592 | bytes 479232
  13.3 1.6 %bitcast_dynamic-update-slice_fusion.23 = f32[14,48,768]{2,1,0:T(8,128)} fusion(f32[14,48,768]{2,1,0:T(8,128)} %get-tuple-element.111, pred[48,768]{1,0:T(8,128)(4,1)S(1)} %get-tuple-element.112, f32[3,48,768]{2,1,0:T(8,128)} %param.7), kind=kLoop, calls=%fused_computation.1752 | loop fusion | flops 73728 | bytes 331776
  14.8 1.6 %bitcast_dynamic-update-slice_fusion.22 = f32[14,48,768]{2,1,0:T(8,128)} fusion(f32[14,48,768]{2,1,0:T(8,128)} %bitcast_dynamic-update-slice_fusion.23, pred[48,768]{1,0:T(8,128)(4,1)S(1)} %get-tuple-element.112, f32[3,48,768]{2,1,0:T(8,128)} %param.7), kind=kLoop, calls=%fused_computation.1747 | loop fusion | flops 73728 | bytes 331776
  18.1 3.0 %collective-permute-start.3 = (f32[1,50,16]{2,1,0:T(8,128)S(1)}, f32[1,50,16]{2,1,0:T(8,128)S(1)}, u32[]{:S(2)}, u32[]{:S(2)}) collective-permute-start(f32[1,50,16]{2,1,0:T(8,128)S(1)} %get-tuple-element.127), channel_id=1, source_target_pairs={{0,1},{2,3},{4,5},{6,7},{8,9},{10,11},{12,13},{14,15},{16,17},{18,... | collective-permute-start | bytes 9608 | tf_op jit(solution)/shard_map/ppermute | solution.py:46
  22.1 1.8 %bitcast_dynamic-update-slice_fusion.21 = (f32[14,48,768]{2,1,0:T(8,128)}, f32[48,768]{1,0:T(8,128)S(1)}, f32[48,768]{1,0:T(8,128)S(1)}, f32[48,768]{1,0:T(8,128)S(1)}, f32[48,768]{1,0:T(8,128)S(1)}) fusion(f32[14,48,768]{2,1,0:T(8,128)} %bitcast_dynamic-update-slice_fusion.22, pred[48,768]{1,0:T(8,128)(4,1)S(1)} %get-tuple-element.112, ...), kind=kLoop, calls=%fused_computation.1742 | loop fusion | flops 5234688 | bytes 2046464
  31.7 4.5 %collective-permute-start.4 = (f32[14,1,768]{2,1,0:T(1,128)S(1)}, f32[14,1,768]{2,1,0:T(1,128)S(1)}, u32[]{:S(2)}, u32[]{:S(2)}) collective-permute-start(f32[14,1,768]{2,1,0:T(1,128)S(1)} %get-tuple-element.124), channel_id=1, source_target_pairs={{0,2},{2,4},{4,6},{6,8},{8,10},{10,12},{12,14},{1,3},{3,5},{5,7},{... | collective-permute-start | bytes 129032 | tf_op jit(solution)/shard_map/ppermute | solution.py:46
  37.9 1.9 %maximum_maximum_fusion = f32[14,50,768]{2,1,0:T(8,128)S(1)} fusion(f32[14,48,768]{2,1,0:T(8,128)} %bitcast_dynamic-update-slice_fusion.12, f32[14,1,768]{2,1,0:T(1,128)S(1)} %collective-permute-done.4, f32[50]{0:T(128)S(1)} %pad.60.clone), kind=kLoop, calls=%fused_computation.511 | loop fusion | flops 1075200 | bytes 4257992 | tf_op jit(solution)/shard_map/concatenate | solution.py:218
  39.8 2.8 %collective-permute-done.5 = f32[14,1,768]{2,1,0:T(1,128)S(1)} collective-permute-done((f32[14,1,768]{2,1,0:T(1,128)S(1)}, f32[14,1,768]{2,1,0:T(1,128)S(1)}, u32[]{:S(2)}, u32[]{:S(2)}) %collective-permute-start.5) | collective-permute-done | bytes 43040 | tf_op jit(solution)/shard_map/ppermute | solution.py:48
  42.6 1.5 %dynamic_update_slice.13 = f32[14,50,768]{2,1,0:T(8,128)S(1)} dynamic-update-slice(f32[14,50,768]{2,1,0:T(8,128)S(1)} %maximum_maximum_fusion, f32[14,1,768]{2,1,0:T(1,128)S(1)} %collective-permute-done.5, s32[]{:T(128)} %constant.462.clone.1, s32[]{:T(128)S(6)} %select_n.1110, s32[]{:T(128)} %constant.462.clone.1) | dynamic-update-slice | bytes 86020 | tf_op jit(solution)/shard_map/dynamic_update_slice | solution.py:219
  45.5 3.1 %collective-permute-start.6 = (f32[14,50,16]{2,1,0:T(8,128)S(1)}, f32[14,50,16]{2,1,0:T(8,128)S(1)}, u32[]{:S(2)}, u32[]{:S(2)}) collective-permute-start(f32[14,50,16]{2,1,0:T(8,128)S(1)} %get-tuple-element.119), channel_id=1, source_target_pairs={{0,1},{2,3},{4,5},{6,7},{8,9},{10,11},{12,13},{14,15},{16,17},{18,... | collective-permute-start | bytes 134408 | tf_op jit(solution)/shard_map/ppermute | solution.py:46
  51.1 1.9 %fusion.420 = (f32[48,768]{1,0:T(8,128)S(1)}, f32[1,48,768]{2,1,0:T(8,128)S(1)}, f32[1,48,768]{2,1,0:T(8,128)S(1)}) fusion(f32[14,50,768]{2,1,0:T(8,128)S(1)} %dynamic_update_slice.13, pred[768]{0:T(1024)(128)(4,1)S(1)} %get-tuple-element.136, pred[768]{0:T(1024)(128)(4,1)S(1)} %get-tuple-element.137, pred[768]{0:T(1024)(128)(4,1)S(1)} %get-tuple-element.138, ...), kind=kLoop, calls=%fused_computation.1157 | loop fusion | flops 7852032 | bytes 5728768 | tf_op jit(solution)/shard_map/add | solution.py:159
  53.0 6.7 %add_add_fusion.4 = (f32[48,768]{1,0:T(8,128)S(1)}, f32[48,768]{1,0:T(8,128)}, f32[48,768]{1,0:T(8,128)}, f32[48,768]{1,0:T(8,128)}, f32[48,768]{1,0:T(8,128)S(1...) fusion(f32[14,50,768]{2,1,0:T(8,128)S(1)} %dynamic_update_slice, ...), kind=kLoop, calls=%fused_computation.1793 | loop fusion | flops 17473536 | bytes 13986304 | tf_op jit(solution)/shard_map/add | solution.py:155
  59.7 3.9 %multiply_subtract_fusion = (f32[1,48,768]{2,1,0:T(8,128)S(1)}, f32[1,48,768]{2,1,0:T(8,128)}, f32[1,48,768]{2,1,0:T(8,128)S(1)}) fusion(f32[1,48,768]{2,1,0:T(8,128)S(1)} %get-tuple-element.55, pred[768]{0:T(1024)(128)(4,1)S(1)} %get-tuple-element.137, f32[1,48,768]{2,1,0:T(8,128)S(1)} %get-tuple-element.56, pred[768]{0:T(1024)(128)(4,1)S(1)} %get-tuple-element.136, ...), kind=kLoop, calls=%fused_computation.1792 | loop fusion | flops 13234176 | bytes 10152448 | tf_op jit(solution)/shard_map/sub | solution.py:288
  64.3 4.8 %collective-permute-start.8 = (f32[1,1,768]{2,1,0:T(1,128)S(1)}, f32[1,1,768]{2,1,0:T(1,128)S(1)}, u32[]{:S(2)}, u32[]{:S(2)}) collective-permute-start(f32[1,1,768]{2,1,0:T(1,128)S(1)} %fusion.826), channel_id=1, source_target_pairs={{0,2},{2,4},{4,6},{6,8},{8,10},{10,12},{12,14},{1,3},{3,5},{5,7},{... | collective-permute-start | bytes 9224 | tf_op jit(solution)/shard_map/ppermute | solution.py:46
  69.1 1.3 %collective-permute-start.9 = (f32[1,1,768]{2,1,0:T(1,128)S(1)}, f32[1,1,768]{2,1,0:T(1,128)S(1)}, u32[]{:S(2)}, u32[]{:S(2)}) collective-permute-start(f32[1,1,768]{2,1,0:T(1,128)S(1)} %slice.2551), channel_id=1, source_target_pairs={{2,0},{4,2},{6,4},{8,6},{10,8},{12,10},{14,12},{3,1},{5,3},{7,5},{... | collective-permute-start | bytes 9224 | tf_op jit(solution)/shard_map/ppermute | solution.py:48
  72.2 2.5 %collective-permute-done.9 = f32[1,1,768]{2,1,0:T(1,128)S(1)} collective-permute-done((f32[1,1,768]{2,1,0:T(1,128)S(1)}, f32[1,1,768]{2,1,0:T(1,128)S(1)}, u32[]{:S(2)}, u32[]{:S(2)}) %collective-permute-start.9) | collective-permute-done | bytes 3104 | tf_op jit(solution)/shard_map/ppermute | solution.py:48
  76.1 3.2 %collective-permute-start.11 = (f32[1,50,16]{2,1,0:T(8,128)S(1)}, f32[1,50,16]{2,1,0:T(8,128)S(1)}, u32[]{:S(2)}, u32[]{:S(2)}) collective-permute-start(f32[1,50,16]{2,1,0:T(8,128)S(1)} %get-tuple-element.125), channel_id=1, source_target_pairs={{0,1},{2,3},{4,5},{6,7},{8,9},{10,11},{12,13},{14,15},{16,17},{18,... | collective-permute-start | bytes 9608 | tf_op jit(solution)/shard_map/ppermute | solution.py:46
  79.3 1.7 %bitcast_dynamic-update-slice_fusion.9 = (f32[14,48,768]{2,1,0:T(8,128)}, f32[48,768]{1,0:T(8,128)S(1)}) fusion(f32[14,48,768]{2,1,0:T(8,128)} %get-tuple-element.100, pred[48,768]{1,0:T(8,128)(4,1)S(1)} %get-tuple-element.112, f32[48,768]{1,0:T(8,128)S(1)} %get-tuple-element.62, f32[48,768]{1,0:T(8,128)S(1)} %get-tuple-element.66, ...), kind=kLoop, calls=%fused_computation.1605 | loop fusion | flops 589824 | bytes 1806336
  81.3 2.9 %bitcast_dynamic-update-slice_fusion.8 = (f32[14,48,768]{2,1,0:T(8,128)}, f32[48,768]{1,0:T(8,128)S(1)}, f32[48,768]{1,0:T(8,128)S(1)}, f32[48,768]{1,0:T(8,128)S(1)}, f32[48,768]{1,0:T(8,128)S(1)}) fusion(f32[14,48,768]{2,1,0:T(8,128)} %get-tuple-element.98, pred[48,768]{1,0:T(8,128)(4,1)S(1)} %get-tuple-element.112, ...), kind=kLoop, calls=%fused_computation.1569 | loop fusion | flops 6672384 | bytes 4700672
  92.5 2.9 %collective-permute-start.12 = (f32[14,1,768]{2,1,0:T(1,128)S(1)}, f32[14,1,768]{2,1,0:T(1,128)S(1)}, u32[]{:S(2)}, u32[]{:S(2)}) collective-permute-start(f32[14,1,768]{2,1,0:T(1,128)S(1)} %get-tuple-element.122), channel_id=1, source_target_pairs={{0,2},{2,4},{4,6},{6,8},{8,10},{10,12},{12,14},{1,3},{3,5},{5,7},{... | collective-permute-start | bytes 129032 | tf_op jit(solution)/shard_map/ppermute | solution.py:46
  97.1 1.9 %maximum_maximum_fusion.1 = f32[14,50,768]{2,1,0:T(8,128)S(1)} fusion(f32[14,48,768]{2,1,0:T(8,128)} %bitcast_dynamic-update-slice_fusion, f32[14,1,768]{2,1,0:T(1,128)S(1)} %collective-permute-done.12, f32[50]{0:T(128)S(1)} %pad.60.clone), kind=kLoop, calls=%fused_computation.512 | loop fusion | flops 1075200 | bytes 4257992 | tf_op jit(solution)/shard_map/concatenate | solution.py:218
  99.0 2.4 %collective-permute-done.13 = f32[14,1,768]{2,1,0:T(1,128)S(1)} collective-permute-done((f32[14,1,768]{2,1,0:T(1,128)S(1)}, f32[14,1,768]{2,1,0:T(1,128)S(1)}, u32[]{:S(2)}, u32[]{:S(2)}) %collective-permute-start.13) | collective-permute-done | bytes 43040 | tf_op jit(solution)/shard_map/ppermute | solution.py:48
  101.4 1.5 %dynamic_update_slice.15 = f32[14,50,768]{2,1,0:T(8,128)S(1)} dynamic-update-slice(f32[14,50,768]{2,1,0:T(8,128)S(1)} %maximum_maximum_fusion.1, f32[14,1,768]{2,1,0:T(1,128)S(1)} %collective-permute-done.13, s32[]{:T(128)} %constant.462.clone.1, s32[]{:T(128)S(6)} %select_n.1110, s32[]{:T(128)} %constant.462.clone.1) | dynamic-update-slice | bytes 86020 | tf_op jit(solution)/shard_map/dynamic_update_slice | solution.py:219
  103.0 1.3 %collective-permute-start.14 = (f32[14,50,16]{2,1,0:T(8,128)S(1)}, f32[14,50,16]{2,1,0:T(8,128)S(1)}, u32[]{:S(2)}, u32[]{:S(2)}) collective-permute-start(f32[14,50,16]{2,1,0:T(8,128)S(1)} %get-tuple-element.114), channel_id=1, source_target_pairs={{0,1},{2,3},{4,5},{6,7},{8,9},{10,11},{12,13},{14,15},{16,17},{18,... | collective-permute-start | bytes 134408 | tf_op jit(solution)/shard_map/ppermute | solution.py:46
  104.3 1.3 %collective-permute-start.15 = (f32[14,50,16]{2,1,0:T(8,128)S(1)}, f32[14,50,16]{2,1,0:T(8,128)S(1)}, u32[]{:S(2)}, u32[]{:S(2)}) collective-permute-start(f32[14,50,16]{2,1,0:T(8,128)S(1)} %get-tuple-element.113), channel_id=1, source_target_pairs={{1,0},{3,2},{5,4},{7,6},{9,8},{11,10},{13,12},{15,14},{17,16},{19,... | collective-permute-start | bytes 134408 | tf_op jit(solution)/shard_map/ppermute | solution.py:48
  105.7 2.3 %collective-permute-done.15 = f32[14,50,16]{2,1,0:T(8,128)S(1)} collective-permute-done((f32[14,50,16]{2,1,0:T(8,128)S(1)}, f32[14,50,16]{2,1,0:T(8,128)S(1)}, u32[]{:S(2)}, u32[]{:S(2)}) %collective-permute-start.15) | collective-permute-done | bytes 44832 | tf_op jit(solution)/shard_map/ppermute | solution.py:48
  109.1 6.2 %select_dynamic-update-slice_fusion.5 = (f32[6,48,768]{2,1,0:T(8,128)S(1)}, f32[1,48,768]{2,1,0:T(8,128)S(1)}, f32[1,48,768]{2,1,0:T(8,128)S(1)}, f32[1,48,768]{...) fusion(pred[48]{0:T(512)(128)(4,1)S(1)} %iota_compare_fusion.4,, ...), kind=kLoop, calls=%fused_computation.1783 | loop fusion | flops 18763776 | bytes 14134272
  117.0 1.7 %fusion.786 = f32[48,768]{1,0:T(8,128)} fusion(f32[1,48,768]{2,1,0:T(8,128)S(1)} %get-tuple-element.46, f32[1,48,768]{2,1,0:T(8,128)S(1)} %get-tuple-element.45, f32[1,48,768]{2,1,0:T(8,128)S(1)} %get-tuple-element.44, f32[1,48,768]{2,1,0:T(8,128)S(1)} %get-tuple-element.43, f32[1,48,768]{2,1,0:T(8,128)S(1)} %get-tuple-element.42, ...), kind=kLoop, calls=%fused_computation.1827 | loop fusion | flops 6598656 | bytes 4283328 | tf_op jit(solution)/shard_map/jit(_where)/select_n | solution.py:317
  118.7 2.6 %fusion.787 = f32[48,768]{1,0:T(8,128)} fusion(f32[14,50,16]{2,1,0:T(8,128)S(1)} %collective-permute-done.15, f32[14,50,768]{2,1,0:T(8,128)S(1)} %dynamic_update_slice.15, f32[14,50,16]{2,1,0:T(8,128)S(1)} %collective-permute-done.14, f32[14,50,802]{2,1,0:T(8,128)S(1)} %select_maximum_fusion, pred[48]{0:T(512)(128)(4,1)S(1)} %iota_compare_fusion.4, ...), kind=kLoop, calls=%fused_computation.1828 | loop fusion | flops 7888896 | bytes 5434368 | tf_op jit(solution)/shard_map/jit(_where)/select_n | solution.py:317
  (137 shorter events, 35.1 us)
Async XLA Ops:
  0.6 21.5 %copy-start = (f32[3,48,768]{2,1,0:T(8,128)S(1)}, f32[3,48,768]{2,1,0:T(8,128)}, u32[]{:S(2)}) copy-start(f32[3,48,768]{2,1,0:T(8,128)} %param.7) | copy-start | bytes 1327108
  0.6 21.5 %copy-start.24 = (f32[6,48,768]{2,1,0:T(8,128)S(1)}, f32[6,48,768]{2,1,0:T(8,128)}, u32[]{:S(2)}) copy-start(f32[6,48,768]{2,1,0:T(8,128)} %param.8) | copy-start | bytes 2654212
  3.7 12.8 %collective-permute-start = (f32[1,1,768]{2,1,0:T(1,128)S(1)}, f32[1,1,768]{2,1,0:T(1,128)S(1)}, u32[]{:S(2)}, u32[]{:S(2)}) collective-permute-start(f32[1,1,768]{2,1,0:T(1,128)S(1)} %dynamic-slice_bitcast_fusion), channel_id=1, source_target_pairs={{0,2},{2,4},{4,6},{6,8},{8,10},{10,12},{12,14},{1,3},{3,5},{5,7},{... | collective-permute-start | bytes 9224 | tf_op jit(solution)/shard_map/ppermute | solution.py:46
  8.6 8.0 %collective-permute-start.1 = (f32[1,1,768]{2,1,0:T(1,128)S(1)}, f32[1,1,768]{2,1,0:T(1,128)S(1)}, u32[]{:S(2)}, u32[]{:S(2)}) collective-permute-start(f32[1,1,768]{2,1,0:T(1,128)S(1)} %slice.2216), channel_id=1, source_target_pairs={{2,0},{4,2},{6,4},{8,6},{10,8},{12,10},{14,12},{3,1},{5,3},{7,5},{... | collective-permute-start | bytes 9224 | tf_op jit(solution)/shard_map/ppermute | solution.py:48
  16.8 4.3 %collective-permute-start.2 = (f32[1,50,16]{2,1,0:T(8,128)S(1)}, f32[1,50,16]{2,1,0:T(8,128)S(1)}, u32[]{:S(2)}, u32[]{:S(2)}) collective-permute-start(f32[1,50,16]{2,1,0:T(8,128)S(1)} %get-tuple-element.128), channel_id=1, source_target_pairs={{1,0},{3,2},{5,4},{7,6},{9,8},{11,10},{13,12},{15,14},{17,16},{19,... | collective-permute-start | bytes 9608 | tf_op jit(solution)/shard_map/ppermute | solution.py:48
  18.1 3.9 %collective-permute-start.3 = (f32[1,50,16]{2,1,0:T(8,128)S(1)}, f32[1,50,16]{2,1,0:T(8,128)S(1)}, u32[]{:S(2)}, u32[]{:S(2)}) collective-permute-start(f32[1,50,16]{2,1,0:T(8,128)S(1)} %get-tuple-element.127), channel_id=1, source_target_pairs={{0,1},{2,3},{4,5},{6,7},{8,9},{10,11},{12,13},{14,15},{16,17},{18,... | collective-permute-start | bytes 9608 | tf_op jit(solution)/shard_map/ppermute | solution.py:46
  31.7 6.2 %collective-permute-start.4 = (f32[14,1,768]{2,1,0:T(1,128)S(1)}, f32[14,1,768]{2,1,0:T(1,128)S(1)}, u32[]{:S(2)}, u32[]{:S(2)}) collective-permute-start(f32[14,1,768]{2,1,0:T(1,128)S(1)} %get-tuple-element.124), channel_id=1, source_target_pairs={{0,2},{2,4},{4,6},{6,8},{8,10},{10,12},{12,14},{1,3},{3,5},{5,7},{... | collective-permute-start | bytes 129032 | tf_op jit(solution)/shard_map/ppermute | solution.py:46
  36.3 6.3 %collective-permute-start.5 = (f32[14,1,768]{2,1,0:T(1,128)S(1)}, f32[14,1,768]{2,1,0:T(1,128)S(1)}, u32[]{:S(2)}, u32[]{:S(2)}) collective-permute-start(f32[14,1,768]{2,1,0:T(1,128)S(1)} %get-tuple-element.123), channel_id=1, source_target_pairs={{2,0},{4,2},{6,4},{8,6},{10,8},{12,10},{14,12},{3,1},{5,3},{7,5},{... | collective-permute-start | bytes 129032 | tf_op jit(solution)/shard_map/ppermute | solution.py:48
  44.3 4.4 %collective-permute-start.7 = (f32[14,50,16]{2,1,0:T(8,128)S(1)}, f32[14,50,16]{2,1,0:T(8,128)S(1)}, u32[]{:S(2)}, u32[]{:S(2)}) collective-permute-start(f32[14,50,16]{2,1,0:T(8,128)S(1)} %get-tuple-element.120), channel_id=1, source_target_pairs={{1,0},{3,2},{5,4},{7,6},{9,8},{11,10},{13,12},{15,14},{17,16},{19,... | collective-permute-start | bytes 134408 | tf_op jit(solution)/shard_map/ppermute | solution.py:48
  45.5 4.4 %collective-permute-start.6 = (f32[14,50,16]{2,1,0:T(8,128)S(1)}, f32[14,50,16]{2,1,0:T(8,128)S(1)}, u32[]{:S(2)}, u32[]{:S(2)}) collective-permute-start(f32[14,50,16]{2,1,0:T(8,128)S(1)} %get-tuple-element.119), channel_id=1, source_target_pairs={{0,1},{2,3},{4,5},{6,7},{8,9},{10,11},{12,13},{14,15},{16,17},{18,... | collective-permute-start | bytes 134408 | tf_op jit(solution)/shard_map/ppermute | solution.py:46
  53.0 11.3 %copy-start.25 = (f32[48,768]{1,0:T(8,128)}, f32[48,768]{1,0:T(8,128)S(1)}, u32[]{:S(2)}) copy-start(f32[48,768]{1,0:T(8,128)S(1)} %get-tuple-element.54) | copy-start | bytes 442372
  59.7 10.8 %copy-start.17 = (f32[48,768]{1,0:T(8,128)}, f32[48,768]{1,0:T(8,128)S(1)}, u32[]{:S(2)}) copy-start(f32[48,768]{1,0:T(8,128)S(1)} %get-tuple-element.71) | copy-start | bytes 442372
  59.7 10.8 %copy-start.19 = (f32[48,768]{1,0:T(8,128)}, f32[48,768]{1,0:T(8,128)S(1)}, u32[]{:S(2)}) copy-start(f32[48,768]{1,0:T(8,128)S(1)} %get-tuple-element.72) | copy-start | bytes 442372
  59.7 11.6 %copy-start.3 = (f32[48,768]{1,0:T(8,128)}, f32[48,768]{1,0:T(8,128)S(1)}, u32[]{:S(2)}) copy-start(f32[48,768]{1,0:T(8,128)S(1)} %get-tuple-element.67) | copy-start | bytes 442372
  59.7 11.6 %copy-start.5 = (f32[48,768]{1,0:T(8,128)}, f32[48,768]{1,0:T(8,128)S(1)}, u32[]{:S(2)}) copy-start(f32[48,768]{1,0:T(8,128)S(1)} %get-tuple-element.68) | copy-start | bytes 442372
  59.7 11.6 %copy-start.7 = (f32[48,768]{1,0:T(8,128)}, f32[48,768]{1,0:T(8,128)S(1)}, u32[]{:S(2)}) copy-start(f32[48,768]{1,0:T(8,128)S(1)} %get-tuple-element.73) | copy-start | bytes 442372
  59.7 11.6 %copy-start.9 = (f32[48,768]{1,0:T(8,128)}, f32[48,768]{1,0:T(8,128)S(1)}, u32[]{:S(2)}) copy-start(f32[48,768]{1,0:T(8,128)S(1)} %get-tuple-element.74) | copy-start | bytes 442372
  59.7 11.6 %copy-start.13 = (f32[48,768]{1,0:T(8,128)}, f32[48,768]{1,0:T(8,128)S(1)}, u32[]{:S(2)}) copy-start(f32[48,768]{1,0:T(8,128)S(1)} %get-tuple-element.63) | copy-start | bytes 442372
  59.7 11.6 %copy-start.15 = (f32[48,768]{1,0:T(8,128)}, f32[48,768]{1,0:T(8,128)S(1)}, u32[]{:S(2)}) copy-start(f32[48,768]{1,0:T(8,128)S(1)} %get-tuple-element.64) | copy-start | bytes 442372
  59.7 12.4 %copy-start.1 = (f32[48,768]{1,0:T(8,128)}, f32[48,768]{1,0:T(8,128)S(1)}, u32[]{:S(2)}) copy-start(f32[48,768]{1,0:T(8,128)S(1)} %get-tuple-element.76) | copy-start | bytes 442372
  63.6 15.7 %copy-start.11 = (f32[48,768]{1,0:T(8,128)S(1)}, f32[48,768]{1,0:T(8,128)}, u32[]{:S(2)}) copy-start(f32[48,768]{1,0:T(8,128)} %get-tuple-element.59) | copy-start | bytes 442372
  63.6 15.7 %copy-start.12 = (f32[48,768]{1,0:T(8,128)S(1)}, f32[48,768]{1,0:T(8,128)}, u32[]{:S(2)}) copy-start(f32[48,768]{1,0:T(8,128)} %get-tuple-element.60) | copy-start | bytes 442372
  64.3 7.8 %collective-permute-start.8 = (f32[1,1,768]{2,1,0:T(1,128)S(1)}, f32[1,1,768]{2,1,0:T(1,128)S(1)}, u32[]{:S(2)}, u32[]{:S(2)}) collective-permute-start(f32[1,1,768]{2,1,0:T(1,128)S(1)} %fusion.826), channel_id=1, source_target_pairs={{0,2},{2,4},{4,6},{6,8},{8,10},{10,12},{12,14},{1,3},{3,5},{5,7},{... | collective-permute-start | bytes 9224 | tf_op jit(solution)/shard_map/ppermute | solution.py:46
  69.1 5.5 %collective-permute-start.9 = (f32[1,1,768]{2,1,0:T(1,128)S(1)}, f32[1,1,768]{2,1,0:T(1,128)S(1)}, u32[]{:S(2)}, u32[]{:S(2)}) collective-permute-start(f32[1,1,768]{2,1,0:T(1,128)S(1)} %slice.2551), channel_id=1, source_target_pairs={{2,0},{4,2},{6,4},{8,6},{10,8},{12,10},{14,12},{3,1},{5,3},{7,5},{... | collective-permute-start | bytes 9224 | tf_op jit(solution)/shard_map/ppermute | solution.py:48
  71.2 9.9 %copy-start.18 = (f32[48,768]{1,0:T(8,128)S(1)}, f32[48,768]{1,0:T(8,128)}, u32[]{:S(2)}) copy-start(f32[48,768]{1,0:T(8,128)} %copy-done.17) | copy-start | bytes 442372
  72.0 9.2 %copy-start.14 = (f32[48,768]{1,0:T(8,128)S(1)}, f32[48,768]{1,0:T(8,128)}, u32[]{:S(2)}) copy-start(f32[48,768]{1,0:T(8,128)} %copy-done.13) | copy-start | bytes 442372
  74.8 6.2 %collective-permute-start.10 = (f32[1,50,16]{2,1,0:T(8,128)S(1)}, f32[1,50,16]{2,1,0:T(8,128)S(1)}, u32[]{:S(2)}, u32[]{:S(2)}) collective-permute-start(f32[1,50,16]{2,1,0:T(8,128)S(1)} %get-tuple-element.126), channel_id=1, source_target_pairs={{1,0},{3,2},{5,4},{7,6},{9,8},{11,10},{13,12},{15,14},{17,16},{19,... | collective-permute-start | bytes 9608 | tf_op jit(solution)/shard_map/ppermute | solution.py:48
  76.1 4.9 %collective-permute-start.11 = (f32[1,50,16]{2,1,0:T(8,128)S(1)}, f32[1,50,16]{2,1,0:T(8,128)S(1)}, u32[]{:S(2)}, u32[]{:S(2)}) collective-permute-start(f32[1,50,16]{2,1,0:T(8,128)S(1)} %get-tuple-element.125), channel_id=1, source_target_pairs={{0,1},{2,3},{4,5},{6,7},{8,9},{10,11},{12,13},{14,15},{16,17},{18,... | collective-permute-start | bytes 9608 | tf_op jit(solution)/shard_map/ppermute | solution.py:46
  92.5 4.6 %collective-permute-start.12 = (f32[14,1,768]{2,1,0:T(1,128)S(1)}, f32[14,1,768]{2,1,0:T(1,128)S(1)}, u32[]{:S(2)}, u32[]{:S(2)}) collective-permute-start(f32[14,1,768]{2,1,0:T(1,128)S(1)} %get-tuple-element.122), channel_id=1, source_target_pairs={{0,2},{2,4},{4,6},{6,8},{8,10},{10,12},{12,14},{1,3},{3,5},{5,7},{... | collective-permute-start | bytes 129032 | tf_op jit(solution)/shard_map/ppermute | solution.py:46
  95.4 5.9 %collective-permute-start.13 = (f32[14,1,768]{2,1,0:T(1,128)S(1)}, f32[14,1,768]{2,1,0:T(1,128)S(1)}, u32[]{:S(2)}, u32[]{:S(2)}) collective-permute-start(f32[14,1,768]{2,1,0:T(1,128)S(1)} %get-tuple-element.121), channel_id=1, source_target_pairs={{2,0},{4,2},{6,4},{8,6},{10,8},{12,10},{14,12},{3,1},{5,3},{7,5},{... | collective-permute-start | bytes 129032 | tf_op jit(solution)/shard_map/ppermute | solution.py:48
  103.0 2.7 %collective-permute-start.14 = (f32[14,50,16]{2,1,0:T(8,128)S(1)}, f32[14,50,16]{2,1,0:T(8,128)S(1)}, u32[]{:S(2)}, u32[]{:S(2)}) collective-permute-start(f32[14,50,16]{2,1,0:T(8,128)S(1)} %get-tuple-element.114), channel_id=1, source_target_pairs={{0,1},{2,3},{4,5},{6,7},{8,9},{10,11},{12,13},{14,15},{16,17},{18,... | collective-permute-start | bytes 134408 | tf_op jit(solution)/shard_map/ppermute | solution.py:46
  104.3 3.6 %collective-permute-start.15 = (f32[14,50,16]{2,1,0:T(8,128)S(1)}, f32[14,50,16]{2,1,0:T(8,128)S(1)}, u32[]{:S(2)}, u32[]{:S(2)}) collective-permute-start(f32[14,50,16]{2,1,0:T(8,128)S(1)} %get-tuple-element.113), channel_id=1, source_target_pairs={{1,0},{3,2},{5,4},{7,6},{9,8},{11,10},{13,12},{15,14},{17,16},{19,... | collective-permute-start | bytes 134408 | tf_op jit(solution)/shard_map/ppermute | solution.py:48
  (15 other events, 86.0 us)
where the time goes:
time: 122 us; the launch traced here: 121 us
  other arithmetic  58.8 us (48%)
  starting transfers between devices  38.1 us (31%)
  waiting for transfers between devices  12.7 us (10%)
  local copies, waits for them, and re-layouts  9.67 us (8%)
  between operations  1.97 us (2%)
    unnamed x27, other arithmetic  30.7 us
    ppermute x8, starting transfers between devices, padded_2(): lax.ppermute(tail, axis, [(i, (i + 1) % count) for i in range(ends)])  27.8 us
    ppermute x8, starting transfers between devices, padded_2(): lax.ppermute(head, axis, [((i + 1) % count, i) for i in range(ends)])  10.3 us
    ppermute x8, waiting for transfers between devices, padded_2(): lax.ppermute(head, axis, [((i + 1) % count, i) for i in range(ends)])  9.91 us
    add x1, other arithmetic, accumulate(): totals[position] + contribution  6.66 us
    sub x2, other arithmetic, shallow_step(): colour = (2.0 * fields[10] - fields[0])[None]  4.87 us
    select_n x2, other arithmetic, body(): results = [jnp.where(row_live, grid, 0.0) for grid in fields]  4.31 us
    concatenate x4, other arithmetic, widen_rows(): jnp.concatenate([received[:, :margin], local_rows, zero_rows], axis=1)  3.9 us
  transfers between devices with their start and end apart: 16, of which 8 were waited for; matrix products, arithmetic and copies ran while one was open for 11% of the time, Pallas kernels for 0%

commit v1 on v0

v1 whole, which is shorter than its diff:
```python
import functools

import jax
import jax.numpy as jnp
from jax import lax
from jax.experimental import pallas as pl
from jax.experimental.pallas import tpu as pltpu
from jax.sharding import PartitionSpec as P

TILE = 16
STEPS = 2
RELAX_TIME = 0.8
SURFACE = 0.1
SEPARATION = 0.7

LANES = 128
SUBLANES = 8
HALO = 4
CELLS_Y = LANES // TILE


def roll_lanes(values, amount):
    return pltpu.roll(values, amount % LANES, 2)


class Geometry:
    def __init__(self, sub_index, own_tiles):
        shape = (1, SUBLANES, LANES)
        lane = lax.broadcasted_iota(jnp.int32, shape, 2)
        tile = lax.broadcasted_iota(jnp.int32, shape, 1)
        depth = lane & (TILE - 1)
        self.z_low = depth == 0
        self.z_high = depth == TILE - 1
        low_part = sub_index == 0
        high_part = sub_index == 1
        self.y_low = (tile == 1) & (lane < TILE) & low_part
        self.y_high = (tile == own_tiles) & (lane >= LANES - TILE) & high_part
        own = (tile >= 1) & (tile <= own_tiles)
        self.domain = own | ((tile == own_tiles + 1) & low_part) | ((tile == 0) & high_part)
        self.first_lanes = lane < TILE
        self.last_lanes = lane >= LANES - TILE

    def from_low_y(self, values, depth_shift=0):
        crossed = jnp.where(self.last_lanes, pltpu.roll(values, 1, 1), values)
        return roll_lanes(crossed, TILE + depth_shift)

    def from_high_y(self, values, depth_shift=0):
        crossed = jnp.where(self.first_lanes, pltpu.roll(values, SUBLANES - 1, 1), values)
        return roll_lanes(crossed, -TILE + depth_shift)

    def from_low_z(self, values):
        return jnp.where(self.z_low, 0.0, roll_lanes(values, 1))

    def from_high_z(self, values):
        return jnp.where(self.z_high, 0.0, roll_lanes(values, -1))


def load_rows(ref, index, row, count):
    start = row * SUBLANES
    if not isinstance(start, int):
        start = pl.multiple_of(start, SUBLANES)
    return ref[index, pl.ds(start, count * SUBLANES), :].reshape(count, SUBLANES, LANES)


def store_rows(ref, index, row, values):
    count = values.shape[0]
    start = row * SUBLANES
    if not isinstance(start, int):
        start = pl.multiple_of(start, SUBLANES)
    ref[index, pl.ds(start, count * SUBLANES), :] = values.reshape(count * SUBLANES, LANES)


def fill_wall_table(walls, geometry):
    one = jnp.ones((1, SUBLANES, LANES), jnp.float32)
    up_y = jnp.where(geometry.y_high, 0.0, one)
    down_y = jnp.where(geometry.y_low, 0.0, one)
    up_z = jnp.where(geometry.z_high, 0.0, one)
    down_z = jnp.where(geometry.z_low, 0.0, one)
    sum_y, sum_z = up_y + down_y, up_z + down_z
    for kind, (up_x, down_x) in enumerate(((1.0, 1.0), (1.0, 0.0), (0.0, 1.0))):
        sum_x = up_x + down_x
        around_x = 2.0 + sum_y + sum_z
        total = 12.0 + 2.0 * (sum_x + sum_y + sum_z) + sum_x * (sum_y + sum_z) + sum_y * sum_z
        rows = (
            (up_x - down_x) * around_x,
            (up_y - down_y) * (2.0 + sum_x + sum_z),
            (up_z - down_z) * (2.0 + sum_x + sum_y),
            36.0 - total,
        )
        for position, row in enumerate(rows):
            store_rows(walls, position, kind, row)


def wall_rows(walls, position, kinds):
    return jnp.concatenate([load_rows(walls, position, kind, 1) for kind in kinds], axis=0)


def colour_pass(fields, colours, geometry, rows, first_row, count, block):
    def step(index, carry):
        row = first_row + index * block
        at = row + HALO
        density = load_rows(fields, 0, at, block)
        red = load_rows(fields, 10, at, block)
        ids = row + lax.broadcasted_iota(jnp.int32, (block, SUBLANES, LANES), 0)
        valid = geometry.domain & (ids >= rows[0]) & (ids < rows[1])
        colour = jnp.where(valid, 2.0 * red - density, 0.0)
        along_y = geometry.from_low_y(colour) + geometry.from_high_y(colour)
        along_z = geometry.from_low_z(colour) + geometry.from_high_z(colour)
        store_rows(colours, 0, at, colour)
        store_rows(colours, 1, at, 2.0 * colour + (along_y + along_z))
        store_rows(colours, 2, at, along_y)
        store_rows(colours, 3, at, along_z)
        return carry

    lax.fori_loop(0, pl.cdiv(count, block), step, 0)


def collide_pass(fields, colours, walls, moved, reds, geometry, rows, first_row, count, block):
    relaxing = 1.0 - 1.0 / RELAX_TIME
    third = 1.0 / 3.0

    def step(index, carry):
        row = first_row + index * block
        at = row + HALO
        kinds = []
        for extra in range(block):
            here = row + extra
            kinds.append(
                jnp.where(here == rows[0], 1, 0) + jnp.where(here == rows[1] - 1, 2, 0)
            )
        colour = load_rows(colours, 0, at, block)
        doubled = 2.0 * colour + (
            load_rows(colours, 0, at - 1, block) + load_rows(colours, 0, at + 1, block)
        )
        term_y = doubled + load_rows(colours, 3, at, block)
        term_z = doubled + load_rows(colours, 2, at, block)
        grad_x = load_rows(colours, 1, at + 1, block) - load_rows(colours, 1, at - 1, block)
        grad_y = geometry.from_high_y(term_y) - geometry.from_low_y(term_y)
        grad_z = geometry.from_high_z(term_z) - geometry.from_low_z(term_z)
        grad_x = (grad_x - wall_rows(walls, 0, kinds) * colour) * (1.0 / 12.0)
        grad_y = (grad_y - wall_rows(walls, 1, kinds) * colour) * (1.0 / 12.0)
        grad_z = (grad_z - wall_rows(walls, 2, kinds) * colour) * (1.0 / 12.0)

        fluid = load_rows(fields, 11, at, block) == 0.0
        density = load_rows(fields, 0, at, block)
        red = load_rows(fields, 10, at, block)
        flux = [load_rows(fields, 1 + axis, at, block) for axis in range(3)]
        stress = [load_rows(fields, 4 + part, at, block) for part in range(6)]
        square_xx, square_yy, square_zz = grad_x * grad_x, grad_y * grad_y, grad_z * grad_z
        square = square_xx + square_yy + square_zz
        inverse = jnp.where(fluid, lax.rsqrt(1.0 + square), 0.0)
        strength = SURFACE * inverse
        keep = jnp.where(fluid, relaxing, 1.0)
        sign = jnp.where(fluid, 1.0, -1.0)
        trace = third * square
        surface = (
            square_xx - trace,
            square_yy - trace,
            square_zz - trace,
            grad_x * grad_y,
            grad_x * grad_z,
            grad_y * grad_z,
        )
        pairs = ((0, 0), (1, 1), (2, 2), (0, 1), (0, 2), (1, 2))
        second = [
            flux[a] * flux[b] + (keep * before + strength * addend)
            for (a, b), before, addend in zip(pairs, stress, surface)
        ]
        flux = [sign * part for part in flux]
        mixing = (SEPARATION * red) * (density - red) * inverse
        charge = [
            0.5 * part + mixing * grad for part, grad in zip(flux, (grad_x, grad_y, grad_z))
        ]

        base = (density - 1.5 * (second[0] + second[1] + second[2])) * (1.0 / 36.0)
        run = [part * (1.0 / 12.0) for part in flux]
        own = [part * 0.125 for part in second[:3]]
        cross = [part * 0.25 for part in second[3:]]
        store_rows(moved, 0, at, 12.0 * base)
        straight = [base + part for part in own]
        for axis in range(3):
            middle = 2.0 * straight[axis]
            swing = 2.0 * run[axis]
            store_rows(moved, 1 + 2 * axis, at, middle + swing)
            store_rows(moved, 2 + 2 * axis, at, middle - swing)
        for plane, (a, b) in enumerate(((0, 1), (0, 2), (1, 2))):
            middle = straight[a] + own[b]
            same, other = middle + cross[plane], middle - cross[plane]
            along, against = run[a] + run[b], run[a] - run[b]
            first = 7 + 4 * plane
            store_rows(moved, first, at, same + along)
            store_rows(moved, first + 1, at, same - along)
            store_rows(moved, first + 2, at, other + against)
            store_rows(moved, first + 3, at, other - against)

        ids = row + lax.broadcasted_iota(jnp.int32, (block, SUBLANES, LANES), 0)
        valid = geometry.domain & (ids >= rows[0]) & (ids < rows[1])
        scale = jnp.where(valid, 1.0 / 12.0, 0.0)
        red_base = red * (scale * third)
        red_run = [part * scale for part in charge]
        store_rows(reds, 0, at, red_base)
        store_rows(reds, 1, at, red_base + red_run[0])
        store_rows(reds, 2, at, red_base - red_run[0])
        store_rows(reds, 3, at, red_run[1])
        store_rows(reds, 4, at, red_run[2])
        return carry

    lax.fori_loop(0, pl.cdiv(count, block), step, 0)


def arrive_pass(fields, walls, moved, reds, geometry, rows, first_row, count, block):
    third = 1.0 / 3.0

    def step(index, carry):
        row = first_row + index * block
        at = row + HALO
        kinds = []
        for extra in range(block):
            here = row + extra
            kinds.append(
                jnp.where(here == rows[0], 1, 0) + jnp.where(here == rows[1] - 1, 2, 0)
            )
        ids = row + lax.broadcasted_iota(jnp.int32, (block, SUBLANES, LANES), 0)
        x_low = ids == rows[0]
        x_high = ids == rows[1] - 1
        own = [None] * 19

        def here(direction):
            if own[direction] is None:
                own[direction] = load_rows(moved, direction, at, block)
            return own[direction]

        def arrived(direction, opposite, velocity):
            vel_x, vel_y, vel_z = velocity
            values = here(direction) if vel_x == 0 else load_rows(moved, direction, at - vel_x, block)
            if vel_y == 1:
                values = geometry.from_low_y(values, vel_z)
            elif vel_y == -1:
                values = geometry.from_high_y(values, vel_z)
            elif vel_z != 0:
                values = roll_lanes(values, vel_z)
            masks = []
            if vel_x != 0:
                masks.append(x_low if vel_x == 1 else x_high)
            if vel_y != 0:
                masks.append(geometry.y_low if vel_y == 1 else geometry.y_high)
            if vel_z != 0:
                masks.append(geometry.z_low if vel_z == 1 else geometry.z_high)
            wall = functools.reduce(lambda one, two: one | two, masks)
            return jnp.where(wall, here(opposite), values)

        rest = here(0)
        sums, diffs = [], []
        for axis in range(3):
            velocity = [0, 0, 0]
            velocity[axis] = 1
            up = arrived(1 + 2 * axis, 2 + 2 * axis, velocity)
            velocity[axis] = -1
            down = arrived(2 + 2 * axis, 1 + 2 * axis, velocity)
            sums.append(up + down)
            diffs.append(up - down)
        total = rest + sums[0] + sums[1] + sums[2]
        cross = []
        for plane, (a, b) in enumerate(((0, 1), (0, 2), (1, 2))):
            first = 7 + 4 * plane
            parts = []
            for offset, (vel_a, vel_b) in enumerate(((1, 1), (-1, -1), (1, -1), (-1, 1))):
                velocity = [0, 0, 0]
                velocity[a], velocity[b] = vel_a, vel_b
                parts.append(arrived(first + offset, first + (offset ^ 1), velocity))
            same, other = parts[0] + parts[1], parts[2] + parts[3]
            along, against = parts[0] - parts[1], parts[2] - parts[3]
            both = same + other
            cross.append(same - other)
            total = total + both
            sums[a], sums[b] = sums[a] + both, sums[b] + both
            diffs[a], diffs[b] = diffs[a] + (along + against), diffs[b] + (along - against)
        shared = third * total
        store_rows(fields, 0, at, total)
        for axis in range(3):
            store_rows(fields, 1 + axis, at, diffs[axis])
            store_rows(fields, 4 + axis, at, sums[axis] - shared - diffs[axis] * diffs[axis])
        for plane, (a, b) in enumerate(((0, 1), (0, 2), (1, 2))):
            store_rows(fields, 7 + plane, at, cross[plane] - diffs[a] * diffs[b])

        red = load_rows(reds, 0, at, block)
        red_x_up = load_rows(reds, 1, at, block)
        red_y = load_rows(reds, 3, at, block)
        red_z = load_rows(reds, 4, at, block)
        from_x = load_rows(reds, 1, at - 1, block) + load_rows(reds, 2, at + 1, block)
        spread = 2.0 * red + from_x
        spread_y = 2.0 * red_y + (load_rows(reds, 3, at - 1, block) + load_rows(reds, 3, at + 1, block))
        spread_z = 2.0 * red_z + (load_rows(reds, 4, at - 1, block) + load_rows(reds, 4, at + 1, block))
        up_y, down_y = red + red_y, red - red_y
        low_y = (
            (spread + spread_y)
            + geometry.from_low_z(up_y + red_z)
            + geometry.from_high_z(up_y - red_z)
        )
        high_y = (
            (spread - spread_y)
            + geometry.from_low_z(down_y + red_z)
            + geometry.from_high_z(down_y - red_z)
        )
        bounced = (
            wall_rows(walls, 3, kinds) * red
            - wall_rows(walls, 0, kinds) * (red_x_up - red)
            - wall_rows(walls, 1, kinds) * red_y
            - wall_rows(walls, 2, kinds) * red_z
        )
        red_total = (
            12.0 * red
            + 2.0 * from_x
            + geometry.from_low_z(spread + spread_z)
            + geometry.from_high_z(spread - spread_z)
            + geometry.from_low_y(low_y)
            + geometry.from_high_y(high_y)
            + bounced
        )
        store_rows(fields, 10, at, red_total)
        return carry

    lax.fori_loop(0, pl.cdiv(count, block), step, 0)


def spread_tiles(source, target, index, own_tiles, row_tiles):
    for row_tile in range(row_tiles):
        for tile in range(own_tiles):
            start = (HALO + row_tile * SUBLANES) * SUBLANES + 1 + tile
            target[index, pl.ds(start, SUBLANES, stride=SUBLANES), :] = source(row_tile, tile)


def steps_kernel(
    info, density, momentum, stress, red, solid, side, low, high,
    density_out, momentum_out, stress_out, red_out,
    fields, colours, walls, moved, reds,
):
    live, first, last, sub_index = info[0], info[1], info[2], info[3]
    row_count, flat_count = density.shape
    own_tiles = flat_count // LANES
    row_tiles = row_count // SUBLANES
    geometry = Geometry(sub_index, own_tiles)
    rows = (jnp.where(first == 1, 0, -1000), jnp.where(last == 1, live, 1000))
    fill_wall_table(walls, geometry)

    sources = [density] + [momentum.at[axis] for axis in range(3)]
    sources = sources + [stress.at[part] for part in range(6)] + [red, solid]
    low_part = sub_index == 0
    for index, source in enumerate(sources):

        def piece(row_tile, tile, source=source):
            values = source[pl.ds(row_tile * SUBLANES, SUBLANES), pl.ds(tile * LANES, LANES)]
            return values.astype(jnp.float32)

        spread_tiles(piece, fields, index, own_tiles, row_tiles)
        for row_tile in range(row_tiles):
            start = (HALO + row_tile * SUBLANES) * SUBLANES
            values = side[index, pl.ds(row_tile * SUBLANES, SUBLANES), :]
            below = jnp.where(low_part, 0.0, values)
            above = jnp.where(low_part, values, 0.0)
            fields[index, pl.ds(start, SUBLANES, stride=SUBLANES), :] = below
            fields[index, pl.ds(start + own_tiles + 1, SUBLANES, stride=SUBLANES), :] = above
        fields[index, pl.ds(0, HALO * SUBLANES), :] = low[index]
        end = pl.multiple_of((HALO + live) * SUBLANES, SUBLANES)
        fields[index, pl.ds(end, HALO * SUBLANES), :] = high[index]

    for repeat in range(STEPS):
        rim = 2 * (STEPS - 1 - repeat)
        colour_pass(fields, colours, geometry, rows, -rim - 2, live + 2 * rim + 4, 4)
        collide_pass(
            fields, colours, walls, moved, reds, geometry, rows, -rim - 1, live + 2 * rim + 2, 2
        )
        arrive_pass(fields, walls, moved, reds, geometry, rows, -rim, live + 2 * rim, 2)

    targets = [density_out] + [momentum_out.at[axis] for axis in range(3)]
    targets = targets + [stress_out.at[part] for part in range(6)] + [red_out]
    for index, target in enumerate(targets):
        for row_tile in range(row_tiles):
            alive = row_tile * SUBLANES < live
            for tile in range(own_tiles):
                start = (HALO + row_tile * SUBLANES) * SUBLANES + 1 + tile
                values = fields[index, pl.ds(start, SUBLANES, stride=SUBLANES), :]
                target[pl.ds(row_tile * SUBLANES, SUBLANES), pl.ds(tile * LANES, LANES)] = (
                    jnp.where(alive, values, 0.0)
                )


def run_steps(info, arrays, side, low, high):
    density = arrays[0]
    row_count, flat_count = density.shape
    scratch_rows = (row_count + 2 * HALO + SUBLANES) * SUBLANES
    shapes = [jax.ShapeDtypeStruct(array.shape, jnp.float32) for array in arrays[:4]]
    return pl.pallas_call(
        steps_kernel,
        out_shape=shapes,
        in_specs=[pl.BlockSpec(memory_space=pltpu.SMEM)]
        + [pl.BlockSpec(memory_space=pltpu.VMEM)] * 8,
        out_specs=[pl.BlockSpec(memory_space=pltpu.VMEM)] * 4,
        scratch_shapes=[
            pltpu.VMEM((12, scratch_rows, LANES), jnp.float32),
            pltpu.VMEM((4, scratch_rows, LANES), jnp.float32),
            pltpu.VMEM((4, 3 * SUBLANES, LANES), jnp.float32),
            pltpu.VMEM((19, scratch_rows, LANES), jnp.float32),
            pltpu.VMEM((5, scratch_rows, LANES), jnp.float32),
        ],
        compiler_params=pltpu.CompilerParams(vmem_limit_bytes=40 * 1024 * 1024),
    )(info, *arrays, side, low, high)


def body(density, momentum, stress, red_density, solid, widths):
    row_count, flat_count = density.shape
    tiles_index = lax.axis_index("tiles")
    tiles_count = lax.axis_size("tiles")
    sub_index = lax.axis_index("sub")
    chosen = lax.iota(jnp.int32, widths.shape[0]) == tiles_index
    live_rows = jnp.sum(jnp.where(chosen, widths, 0)) * TILE
    info = jnp.stack(
        [
            live_rows,
            (tiles_index == 0).astype(jnp.int32),
            (tiles_index == tiles_count - 1).astype(jnp.int32),
            sub_index.astype(jnp.int32),
        ]
    )
    planes = [density[None], momentum, stress, red_density[None], solid.astype(jnp.float32)[None]]
    low_part = sub_index == 0

    edge = jnp.concatenate(
        [jnp.where(low_part, plane[:, :, -LANES:], plane[:, :, :LANES]) for plane in planes], axis=0
    )
    side = lax.ppermute(edge, "sub", [(0, 1), (1, 0)])

    def send_rows(start):
        own = jnp.concatenate(
            [lax.dynamic_slice_in_dim(plane, start, HALO, axis=1) for plane in planes], axis=0
        )
        beside = lax.dynamic_slice_in_dim(side, start, HALO, axis=1)
        below = jnp.where(low_part, 0.0, beside)
        above = jnp.where(low_part, beside, 0.0)
        whole = jnp.concatenate([below, own, above], axis=2)
        return whole.reshape(12, HALO * SUBLANES, LANES)

    ends = tiles_count - 1
    low = lax.ppermute(
        send_rows(live_rows - HALO), "tiles", [(i, i + 1) for i in range(ends)]
    )
    high = lax.ppermute(send_rows(0), "tiles", [(i + 1, i) for i in range(ends)])
    outs = run_steps(
        info, (density, momentum, stress, red_density, solid), side, low, high
    )
    return tuple(outs)


def solution(mesh):
    in_specs = (
        P(("groups", "tiles"), "sub"),
        P(None, ("groups", "tiles"), "sub"),
        P(None, ("groups", "tiles"), "sub"),
        P(("groups", "tiles"), "sub"),
        P(("groups", "tiles"), "sub"),
        P("groups"),
    )
    out_specs = (
        P(("groups", "tiles"), "sub"),
        P(None, ("groups", "tiles"), "sub"),
        P(None, ("groups", "tiles"), "sub"),
        P(("groups", "tiles"), "sub"),
    )
    return jax.shard_map(body, mesh=mesh, in_specs=in_specs, out_specs=out_specs, check_vma=False)
```

time: 122 us -> 42.9 us (0.35)
  the two profiles are of different devices: /device:TPU:0 before, /device:TPU:27 now
where the time goes in v1:
time: 42.9 us; the launch traced here: 42.5 us
  Pallas kernels  18.7 us (44%)
  waiting for transfers between devices  7.57 us (18%)
  starting transfers between devices  7.05 us (16%)
  other arithmetic  4.41 us (10%)
  local copies, waits for them, and re-layouts  3.29 us (8%)
  between operations  1.44 us (3%)
    pallas_call x1, Pallas kernels, run_steps(): pl.pallas_call(steps_kernel, out_shape=shapes, in_specs=[pl.BlockSpec(mem...  18.7 us
    ppermute x1, waiting for transfers between devices, body(): lax.ppermute(send_rows(0), 'tiles', [(i + 1, i) for i in range(ends)])  4.54 us
    ppermute x1, starting transfers between devices, body(): lax.ppermute(send_rows(live_rows - HALO), 'tiles', [(i, i + 1) for i in r...  3.28 us
    unnamed x18, local copies, waits for them, and re-layouts  3.11 us
    ppermute x1, starting transfers between devices, body(): lax.ppermute(send_rows(0), 'tiles', [(i + 1, i) for i in range(ends)])  3.03 us
    ppermute x1, waiting for transfers between devices, body(): lax.ppermute(send_rows(live_rows - HALO), 'tiles', [(i, i + 1) for i in r...  3.03 us
    unnamed x4, other arithmetic  2.54 us
    convert_element_type x1, other arithmetic, body(): solid.astype(jnp.float32)[None]  1.03 us
  transfers between devices with their start and end apart: 3, of which 2 were waited for; matrix products, arithmetic and copies ran while one was open for 5% of the time, Pallas kernels for 0%

profile of v1, /device:TPU:27, one launch (start us, length us, event | category | flops | bytes accessed | tf_op | source)
XLA Modules:
  0.0 42.5 jit_solution(689806124642078721)
XLA Ops:
  0.6 0.0 copy-start.1
  0.6 0.0 copy-start
  0.7 1.0 %fusion.1 = (f32[48,768]{1,0:T(8,128)S(1)}, f32[1,48,768]{2,1,0:T(8,128)S(1)}) fusion(s32[48,768]{1,0:T(8,128)} %solid.1), kind=kLoop, calls=%fused_computation.28 | loop fusion | flops 36864 | bytes 442368 | tf_op jit(solution)/shard_map/convert_element_type | solution.py:425
  1.7 0.8 %constant_dynamic-update-slice_fusion.2 = f32[12,48,128]{2,1,0:T(8,128)S(1)} fusion(f32[1,48,768]{2,1,0:T(8,128)} %bitcast.14, pred[]{:T(512)S(6)} %eq.19), kind=kLoop, calls=%fused_computation.10 | loop fusion | flops 6143 | bytes 73729
  2.5 0.0 copy-done.1
  2.5 1.0 %select_dynamic-update-slice_fusion = f32[12,48,128]{2,1,0:T(8,128)S(1)} fusion(f32[12,48,128]{2,1,0:T(8,128)S(1)} %select_dynamic-update-slice_fusion.1, f32[6,48,768]{2,1,0:T(8,128)} %stress.1, pred[]{:T(512)S(6)} %eq.19), kind=kLoop, calls=%fused_computation.2 | loop fusion | flops 36864 | bytes 442369
  3.5 0.8 %constant_dynamic-update-slice_fusion.1 = f32[12,48,128]{2,1,0:T(8,128)S(1)} fusion(f32[12,48,128]{2,1,0:T(8,128)S(1)} %select_dynamic-update-slice_fusion, f32[1,48,768]{2,1,0:T(8,128)} %bitcast.16, pred[]{:T(512)S(6)} %eq.19), kind=kLoop, calls=%fused_computation.9 | loop fusion | flops 6144 | bytes 73729
  4.3 0.7 %collective-permute-start = (f32[12,48,128]{2,1,0:T(8,128)S(1)}, f32[12,48,128]{2,1,0:T(8,128)S(1)}, u32[]{:S(2)}, u32[]{:S(2)}) collective-permute-start(f32[12,48,128]{2,1,0:T(8,128)S(1)} %constant_dynamic-update-slice_fusion), channel_id=1, source_target_pairs={{0,1},{1,0},{2,3},{3,2},{4,5},{5,4},{6,7},{7,6},{8,9},{9,8},{10,11... | collective-permute-start | bytes 884744 | tf_op jit(solution)/shard_map/ppermute | solution.py:431
  5.0 0.7 %constant_dynamic-update-slice_fusion.8 = f32[12,4,768]{2,1,0:T(4,128)S(1)} fusion(f32[1,48,768]{2,1,0:T(8,128)} %bitcast.15), kind=kLoop, calls=%fused_computation.16 | loop fusion | bytes 24576
  5.7 0.0 copy-start.5
  5.7 0.7 %copy-done.5 = s32[8]{0:T(128)S(1)} copy-done((s32[8]{0:T(128)S(1)}, s32[8]{0:T(128)}, u32[]{:S(2)}) %copy-start.5) | copy-done | bytes 56
  6.4 0.6 %fusion = s32[]{:T(128)} fusion(s32[8]{0:T(128)S(1)} %copy-done.5, s32[]{:T(128)S(6)} %axis_index.23), kind=kLoop, calls=%fused_computation.25 | loop fusion | flops 23 | bytes 40 | tf_op jit(solution)/shard_map/reduce_sum | solution.py:416
  7.7 0.7 %constant_dynamic-update-slice_fusion.5 = f32[12,4,768]{2,1,0:T(4,128)S(1)} fusion(f32[48,768]{1,0:T(8,128)} %density.1, s32[]{:T(128)S(6)} %select_n.76), kind=kLoop, calls=%fused_computation.13 | loop fusion | bytes 24580
  8.5 0.0 copy-done
  8.5 0.0 copy-start.4
  8.5 0.9 %copy-done.4 = f32[48,768]{1,0:T(8,128)S(1)} copy-done((f32[48,768]{1,0:T(8,128)S(1)}, f32[48,768]{1,0:T(8,128)}, u32[]{:S(2)}) %copy-start.4) | copy-done | bytes 147480
  9.4 0.0 collective-permute-done.side
  9.5 0.1 reshape.18
  9.7 0.0 copy-start.2
  9.7 0.0 copy-start.3
  9.7 0.1 reshape.17
  9.8 3.3 %collective-permute-start.1 = (f32[12,32,128]{2,1,0:T(8,128)S(1)}, f32[12,32,128]{2,1,0:T(8,128)S(1)}, u32[]{:S(2)}, u32[]{:S(2)}) collective-permute-start(f32[12,32,128]{2,1,0:T(8,128)S(1)} %reshape.17), channel_id=1, source_target_pairs={{0,2},{2,4},{4,6},{6,8},{8,10},{10,12},{12,14},{1,3},{3,5},{5,7},{... | collective-permute-start | bytes 589832 | tf_op jit(solution)/shard_map/ppermute | solution.py:444
  13.1 3.0 %collective-permute-start.2 = (f32[12,32,128]{2,1,0:T(8,128)S(1)}, f32[12,32,128]{2,1,0:T(8,128)S(1)}, u32[]{:S(2)}, u32[]{:S(2)}) collective-permute-start(f32[12,32,128]{2,1,0:T(8,128)S(1)} %reshape.18), channel_id=1, source_target_pairs={{2,0},{4,2},{6,4},{8,6},{10,8},{12,10},{14,12},{3,1},{5,3},{7,5},{... | collective-permute-start | bytes 589832 | tf_op jit(solution)/shard_map/ppermute | solution.py:447
  16.1 0.1 pad_add_fusion.info
  16.2 3.0 %collective-permute-done.1.low = f32[12,32,128]{2,1,0:T(8,128)S(1)} collective-permute-done((f32[12,32,128]{2,1,0:T(8,128)S(1)}, f32[12,32,128]{2,1,0:T(8,128)S(1)}, u32[]{:S(2)}, u32[]{:S(2)}) %collective-permute-start.1) | collective-permute-done | bytes 196640 | tf_op jit(solution)/shard_map/ppermute | solution.py:444
  19.2 4.5 %collective-permute-done.2.high = f32[12,32,128]{2,1,0:T(8,128)S(1)} collective-permute-done((f32[12,32,128]{2,1,0:T(8,128)S(1)}, f32[12,32,128]{2,1,0:T(8,128)S(1)}, u32[]{:S(2)}, u32[]{:S(2)}) %collective-permute-start.2) | collective-permute-done | bytes 196640 | tf_op jit(solution)/shard_map/ppermute | solution.py:447
  23.8 0.0 copy-done.2
  23.8 0.0 copy-done.3
  23.8 18.7 %shard_map.93 = (f32[48,768]{1,0:T(8,128)}, f32[3,48,768]{2,1,0:T(8,128)}, f32[6,48,768]{2,1,0:T(8,128)}, f32[48,768]{1,0:T(8,128)}) custom-call(s32[4]{0:T(128)S(1)} %pad_add_fusion.info, f32[48,768]{1,0:T(8,128)S(1)} %copy-done.3, f32[3,48,768]{2,1,0:T(8,128)S(1)} %copy-done.1, f32[6,48,768]{2,1,0:T(8,128)S(1)} %copy-done, f32[48,768]{1,0:T(8,128)S(1)} %copy-done.4, ...), custom_call_target="tpu_custom_call" | custom-call | tf_op jit(solution)/shard_map/pallas_call | solution.py:393
  (10 shorter events, 0.2 us)
Async XLA Ops:
  0.6 1.8 %copy-start.1 = (f32[3,48,768]{2,1,0:T(8,128)S(1)}, f32[3,48,768]{2,1,0:T(8,128)}, u32[]{:S(2)}) copy-start(f32[3,48,768]{2,1,0:T(8,128)} %momentum.1) | copy-start | bytes 1327108
  0.6 7.8 %copy-start = (f32[6,48,768]{2,1,0:T(8,128)S(1)}, f32[6,48,768]{2,1,0:T(8,128)}, u32[]{:S(2)}) copy-start(f32[6,48,768]{2,1,0:T(8,128)} %stress.1) | copy-start | bytes 2654212
  4.3 5.2 %collective-permute-start = (f32[12,48,128]{2,1,0:T(8,128)S(1)}, f32[12,48,128]{2,1,0:T(8,128)S(1)}, u32[]{:S(2)}, u32[]{:S(2)}) collective-permute-start(f32[12,48,128]{2,1,0:T(8,128)S(1)} %constant_dynamic-update-slice_fusion), channel_id=1, source_target_pairs={{0,1},{1,0},{2,3},{3,2},{4,5},{5,4},{6,7},{7,6},{8,9},{9,8},{10,11... | collective-permute-start | bytes 884744 | tf_op jit(solution)/shard_map/ppermute | solution.py:431
  5.7 0.7 %copy-start.5 = (s32[8]{0:T(128)S(1)}, s32[8]{0:T(128)}, u32[]{:S(2)}) copy-start(s32[8]{0:T(128)} %param.11) | copy-start | bytes 100
  8.5 0.9 %copy-start.4 = (f32[48,768]{1,0:T(8,128)S(1)}, f32[48,768]{1,0:T(8,128)}, u32[]{:S(2)}) copy-start(f32[48,768]{1,0:T(8,128)} %red.1) | copy-start | bytes 442372
  9.7 14.1 %copy-start.2 = (s32[48,768]{1,0:T(8,128)S(1)}, s32[48,768]{1,0:T(8,128)}, u32[]{:S(2)}) copy-start(s32[48,768]{1,0:T(8,128)} %solid.1) | copy-start | bytes 442372
  9.7 14.1 %copy-start.3 = (f32[48,768]{1,0:T(8,128)S(1)}, f32[48,768]{1,0:T(8,128)}, u32[]{:S(2)}) copy-start(f32[48,768]{1,0:T(8,128)} %density.1) | copy-start | bytes 442372
  9.8 9.5 %collective-permute-start.1 = (f32[12,32,128]{2,1,0:T(8,128)S(1)}, f32[12,32,128]{2,1,0:T(8,128)S(1)}, u32[]{:S(2)}, u32[]{:S(2)}) collective-permute-start(f32[12,32,128]{2,1,0:T(8,128)S(1)} %reshape.17), channel_id=1, source_target_pairs={{0,2},{2,4},{4,6},{6,8},{8,10},{10,12},{12,14},{1,3},{3,5},{5,7},{... | collective-permute-start | bytes 589832 | tf_op jit(solution)/shard_map/ppermute | solution.py:444
  13.1 10.7 %collective-permute-start.2 = (f32[12,32,128]{2,1,0:T(8,128)S(1)}, f32[12,32,128]{2,1,0:T(8,128)S(1)}, u32[]{:S(2)}, u32[]{:S(2)}) collective-permute-start(f32[12,32,128]{2,1,0:T(8,128)S(1)} %reshape.18), channel_id=1, source_target_pairs={{2,0},{4,2},{6,4},{8,6},{10,8},{12,10},{14,12},{3,1},{5,3},{7,5},{... | collective-permute-start | bytes 589832 | tf_op jit(solution)/shard_map/ppermute | solution.py:447

commit v2 on v1

v2 whole, which is shorter than its diff:
```python
import functools

import jax
import jax.numpy as jnp
from jax import lax
from jax.experimental import pallas as pl
from jax.experimental.pallas import tpu as pltpu
from jax.sharding import PartitionSpec as P

TILE = 16
STEPS = 2
RELAX_TIME = 0.8
SURFACE = 0.1
SEPARATION = 0.7

LANES = 128
SUBLANES = 8
FULL = 3
HALO = FULL + 1
FIELDS = 11
PLANES = FIELDS + 1
MOVED = 19
REDS = 5
RIM = 4
SLAB = HALO + 2 * RIM
COLOUR_BLOCK = 8
COLLIDE_BLOCK = 4
ARRIVE_BLOCK = 4
VMEM = pl.BlockSpec(memory_space=pltpu.VMEM)
SMEM = pl.BlockSpec(memory_space=pltpu.SMEM)
ANY = pl.BlockSpec(memory_space=pl.ANY)
HBM = pl.BlockSpec(memory_space=pltpu.HBM)


def roll_lanes(values, amount):
    return pltpu.roll(values, amount % LANES, 2)


class Geometry:
    def __init__(self, info, own_tiles):
        live, first, last, sub_index = info[0], info[1], info[2], info[3]
        self.live = live
        self.low_row = jnp.where(first == 1, 0, -1000)
        self.high_row = jnp.where(last == 1, live, 1000)
        shape = (1, SUBLANES, LANES)
        lane = lax.broadcasted_iota(jnp.int32, shape, 2)
        tile = lax.broadcasted_iota(jnp.int32, shape, 1)
        depth = lane & (TILE - 1)
        self.z_low = depth == 0
        self.z_high = depth == TILE - 1
        low_part = sub_index == 0
        high_part = sub_index == 1
        self.y_low = (tile == 1) & (lane < TILE) & low_part
        self.y_high = (tile == own_tiles) & (lane >= LANES - TILE) & high_part
        own = (tile >= 1) & (tile <= own_tiles)
        self.domain = own | ((tile == own_tiles + 1) & low_part) | ((tile == 0) & high_part)
        self.first_lanes = lane < TILE
        self.last_lanes = lane >= LANES - TILE

    def from_low_y(self, values, depth_shift=0):
        crossed = jnp.where(self.last_lanes, pltpu.roll(values, 1, 1), values)
        return roll_lanes(crossed, TILE + depth_shift)

    def from_high_y(self, values, depth_shift=0):
        crossed = jnp.where(self.first_lanes, pltpu.roll(values, SUBLANES - 1, 1), values)
        return roll_lanes(crossed, -TILE + depth_shift)

    def from_low_z(self, values):
        return jnp.where(self.z_low, 0.0, roll_lanes(values, 1))

    def from_high_z(self, values):
        return jnp.where(self.z_high, 0.0, roll_lanes(values, -1))


def flat_rows(row, count):
    start = row * SUBLANES
    if not isinstance(start, int):
        start = pl.multiple_of(start, SUBLANES)
    return pl.ds(start, count * SUBLANES)


class Block:
    def __init__(self, geometry, spans, inner=False):
        self.spans = spans
        rows = [row + extra for row, local, count in spans for extra in range(count)]
        if inner:
            self.x_low = self.x_high = None
            self.valid = geometry.domain
            self.kinds = [0]
            return
        shape = (1, SUBLANES, LANES)
        ids = jnp.concatenate([row + jnp.zeros(shape, jnp.int32) for row in rows], axis=0)
        self.x_low = ids == geometry.low_row
        self.x_high = ids == geometry.high_row - 1
        self.valid = geometry.domain & (ids >= geometry.low_row) & (ids < geometry.high_row)
        self.kinds = [
            jnp.where(row == geometry.low_row, 1, 0) + jnp.where(row == geometry.high_row - 1, 2, 0)
            for row in rows
        ]

    def load(self, ref, index, offset=0):
        parts = [
            ref[index, flat_rows(local + offset, count), :].reshape(count, SUBLANES, LANES)
            for row, local, count in self.spans
        ]
        return parts[0] if len(parts) == 1 else jnp.concatenate(parts, axis=0)

    def store(self, ref, index, values):
        done = 0
        for row, local, count in self.spans:
            part = values[done : done + count].reshape(count * SUBLANES, LANES)
            ref[index, flat_rows(local, count), :] = part
            done += count

    def walls(self, walls, position):
        parts = [walls[position, flat_rows(kind, 1), :][None] for kind in self.kinds]
        return jnp.concatenate(parts, axis=0)


def fill_wall_table(walls, geometry):
    one = jnp.ones((1, SUBLANES, LANES), jnp.float32)
    up_y = jnp.where(geometry.y_high, 0.0, one)
    down_y = jnp.where(geometry.y_low, 0.0, one)
    up_z = jnp.where(geometry.z_high, 0.0, one)
    down_z = jnp.where(geometry.z_low, 0.0, one)
    sum_y, sum_z = up_y + down_y, up_z + down_z
    for kind, (up_x, down_x) in enumerate(((1.0, 1.0), (1.0, 0.0), (0.0, 1.0))):
        sum_x = up_x + down_x
        around_x = 2.0 + sum_y + sum_z
        total = 12.0 + 2.0 * (sum_x + sum_y + sum_z) + sum_x * (sum_y + sum_z) + sum_y * sum_z
        rows = (
            (up_x - down_x) * around_x,
            (up_y - down_y) * (2.0 + sum_x + sum_z),
            (up_z - down_z) * (2.0 + sum_x + sum_y),
            36.0 - total,
        )
        for position, row in enumerate(rows):
            walls[position, flat_rows(kind, 1), :] = row[0]


def colour_stage(block, geometry, fields, colours):
    density = block.load(fields, 0)
    red = block.load(fields, 10)
    colour = jnp.where(block.valid, 2.0 * red - density, 0.0)
    along_y = geometry.from_low_y(colour) + geometry.from_high_y(colour)
    along_z = geometry.from_low_z(colour) + geometry.from_high_z(colour)
    block.store(colours, 0, colour)
    block.store(colours, 1, 2.0 * colour + (along_y + along_z))
    block.store(colours, 2, along_y)
    block.store(colours, 3, along_z)


def collide_stage(block, geometry, fields, solids, colours, walls, moved, reds):
    relaxing = 1.0 - 1.0 / RELAX_TIME
    third = 1.0 / 3.0
    colour = block.load(colours, 0)
    doubled = 2.0 * colour + (block.load(colours, 0, -1) + block.load(colours, 0, 1))
    term_y = doubled + block.load(colours, 3)
    term_z = doubled + block.load(colours, 2)
    grad_x = block.load(colours, 1, 1) - block.load(colours, 1, -1)
    grad_y = geometry.from_high_y(term_y) - geometry.from_low_y(term_y)
    grad_z = geometry.from_high_z(term_z) - geometry.from_low_z(term_z)
    grad_x = (grad_x - block.walls(walls, 0) * colour) * (1.0 / 12.0)
    grad_y = (grad_y - block.walls(walls, 1) * colour) * (1.0 / 12.0)
    grad_z = (grad_z - block.walls(walls, 2) * colour) * (1.0 / 12.0)

    fluid = block.load(solids, PLANES - 1) == 0.0
    density = block.load(fields, 0)
    red = block.load(fields, 10)
    flux = [block.load(fields, 1 + axis) for axis in range(3)]
    stress = [block.load(fields, 4 + part) for part in range(6)]
    square_xx, square_yy, square_zz = grad_x * grad_x, grad_y * grad_y, grad_z * grad_z
    square = square_xx + square_yy + square_zz
    inverse = jnp.where(fluid, lax.rsqrt(1.0 + square), 0.0)
    strength = SURFACE * inverse
    keep = jnp.where(fluid, relaxing, 1.0)
    sign = jnp.where(fluid, 1.0, -1.0)
    trace = third * square
    surface = (
        square_xx - trace,
        square_yy - trace,
        square_zz - trace,
        grad_x * grad_y,
        grad_x * grad_z,
        grad_y * grad_z,
    )
    pairs = ((0, 0), (1, 1), (2, 2), (0, 1), (0, 2), (1, 2))
    second = [
        flux[a] * flux[b] + (keep * before + strength * addend)
        for (a, b), before, addend in zip(pairs, stress, surface)
    ]
    flux = [sign * part for part in flux]
    mixing = (SEPARATION * red) * (density - red) * inverse
    charge = [0.5 * part + mixing * grad for part, grad in zip(flux, (grad_x, grad_y, grad_z))]

    base = (density - 1.5 * (second[0] + second[1] + second[2])) * (1.0 / 36.0)
    run = [part * (1.0 / 12.0) for part in flux]
    own = [part * 0.125 for part in second[:3]]
    cross = [part * 0.25 for part in second[3:]]
    block.store(moved, 0, 12.0 * base)
    straight = [base + part for part in own]
    for axis in range(3):
        middle = 2.0 * straight[axis]
        swing = 2.0 * run[axis]
        block.store(moved, 1 + 2 * axis, middle + swing)
        block.store(moved, 2 + 2 * axis, middle - swing)
    for plane, (a, b) in enumerate(((0, 1), (0, 2), (1, 2))):
        middle = straight[a] + own[b]
        same, other = middle + cross[plane], middle - cross[plane]
        along, against = run[a] + run[b], run[a] - run[b]
        first = 7 + 4 * plane
        block.store(moved, first, same + along)
        block.store(moved, first + 1, same - along)
        block.store(moved, first + 2, other + against)
        block.store(moved, first + 3, other - against)

    scale = jnp.where(block.valid, 1.0 / 12.0, 0.0)
    red_base = red * (scale * third)
    red_run = [part * scale for part in charge]
    block.store(reds, 0, red_base)
    block.store(reds, 1, red_base + red_run[0])
    block.store(reds, 2, red_base - red_run[0])
    block.store(reds, 3, red_run[1])
    block.store(reds, 4, red_run[2])


def arrive_stage(block, geometry, walls, moved, reds, fields):
    third = 1.0 / 3.0
    own = [None] * MOVED

    def here(direction):
        if own[direction] is None:
            own[direction] = block.load(moved, direction)
        return own[direction]

    def arrived(direction, opposite, velocity):
        vel_x, vel_y, vel_z = velocity
        values = here(direction) if vel_x == 0 else block.load(moved, direction, -vel_x)
        if vel_y == 1:
            values = geometry.from_low_y(values, vel_z)
        elif vel_y == -1:
            values = geometry.from_high_y(values, vel_z)
        elif vel_z != 0:
            values = roll_lanes(values, vel_z)
        masks = []
        if vel_x != 0 and block.x_low is not None:
            masks.append(block.x_low if vel_x == 1 else block.x_high)
        if vel_y != 0:
            masks.append(geometry.y_low if vel_y == 1 else geometry.y_high)
        if vel_z != 0:
            masks.append(geometry.z_low if vel_z == 1 else geometry.z_high)
        if not masks:
            return values
        wall = functools.reduce(lambda one, two: one | two, masks)
        return jnp.where(wall, here(opposite), values)

    rest = here(0)
    sums, diffs = [], []
    for axis in range(3):
        velocity = [0, 0, 0]
        velocity[axis] = 1
        up = arrived(1 + 2 * axis, 2 + 2 * axis, velocity)
        velocity[axis] = -1
        down = arrived(2 + 2 * axis, 1 + 2 * axis, velocity)
        sums.append(up + down)
        diffs.append(up - down)
    total = rest + sums[0] + sums[1] + sums[2]
    cross = []
    for plane, (a, b) in enumerate(((0, 1), (0, 2), (1, 2))):
        first = 7 + 4 * plane
        parts = []
        for offset, (vel_a, vel_b) in enumerate(((1, 1), (-1, -1), (1, -1), (-1, 1))):
            velocity = [0, 0, 0]
            velocity[a], velocity[b] = vel_a, vel_b
            parts.append(arrived(first + offset, first + (offset ^ 1), velocity))
        same, other = parts[0] + parts[1], parts[2] + parts[3]
        along, against = parts[0] - parts[1], parts[2] - parts[3]
        both = same + other
        cross.append(same - other)
        total = total + both
        sums[a], sums[b] = sums[a] + both, sums[b] + both
        diffs[a], diffs[b] = diffs[a] + (along + against), diffs[b] + (along - against)
    shared = third * total
    block.store(fields, 0, total)
    for axis in range(3):
        block.store(fields, 1 + axis, diffs[axis])
        block.store(fields, 4 + axis, sums[axis] - shared - diffs[axis] * diffs[axis])
    for plane, (a, b) in enumerate(((0, 1), (0, 2), (1, 2))):
        block.store(fields, 7 + plane, cross[plane] - diffs[a] * diffs[b])

    red = block.load(reds, 0)
    red_x_up = block.load(reds, 1)
    red_y = block.load(reds, 3)
    red_z = block.load(reds, 4)
    from_x = block.load(reds, 1, -1) + block.load(reds, 2, 1)
    spread = 2.0 * red + from_x
    spread_y = 2.0 * red_y + (block.load(reds, 3, -1) + block.load(reds, 3, 1))
    spread_z = 2.0 * red_z + (block.load(reds, 4, -1) + block.load(reds, 4, 1))
    up_y, down_y = red + red_y, red - red_y
    low_y = (
        (spread + spread_y)
        + geometry.from_low_z(up_y + red_z)
        + geometry.from_high_z(up_y - red_z)
    )
    high_y = (
        (spread - spread_y)
        + geometry.from_low_z(down_y + red_z)
        + geometry.from_high_z(down_y - red_z)
    )
    bounced = (
        block.walls(walls, 3) * red
        - block.walls(walls, 0) * (red_x_up - red)
        - block.walls(walls, 1) * red_y
        - block.walls(walls, 2) * red_z
    )
    red_total = (
        12.0 * red
        + 2.0 * from_x
        + geometry.from_low_z(spread + spread_z)
        + geometry.from_high_z(spread - spread_z)
        + geometry.from_low_y(low_y)
        + geometry.from_high_y(high_y)
        + bounced
    )
    block.store(fields, 10, red_total)


def over_rows(geometry, first, end, size, stage):
    def step(index, carry):
        row = jnp.minimum(first + index * size, end - size)
        stage(Block(geometry, [(row, row, size)], inner=True))
        return carry

    lax.fori_loop(0, (end - first + size - 1) // size, step, 0)


def edge_kernel(density, momentum, stress, red, solid, edge, solid_edge, sems):
    own_tiles = density.shape[1] // LANES
    start = jnp.where(lax.axis_index("sub") == 0, (own_tiles - 1) * LANES, 0)
    lanes = pl.ds(pl.multiple_of(start, LANES), LANES)
    copies = [
        pltpu.make_async_copy(density.at[:, lanes], edge.at[0], sems.at[0]),
        pltpu.make_async_copy(momentum.at[:, :, lanes], edge.at[pl.ds(1, 3)], sems.at[1]),
        pltpu.make_async_copy(stress.at[:, :, lanes], edge.at[pl.ds(4, 6)], sems.at[2]),
        pltpu.make_async_copy(red.at[:, lanes], edge.at[10], sems.at[3]),
        pltpu.make_async_copy(solid.at[:, lanes], solid_edge, sems.at[4]),
    ]
    for copy in copies:
        copy.start()
    for copy in copies:
        copy.wait()
    edge[PLANES - 1] = solid_edge[...].astype(jnp.float32)


def take_edge(arrays):
    row_count = arrays[0].shape[0]
    return pl.pallas_call(
        edge_kernel,
        out_shape=jax.ShapeDtypeStruct((PLANES, row_count, LANES), jnp.float32),
        in_specs=[HBM] * 5,
        out_specs=VMEM,
        scratch_shapes=[pltpu.VMEM((row_count, LANES), jnp.int32), pltpu.SemaphoreType.DMA((5,))],
        name="edge",
    )(*arrays)


def spread_kernel(density, momentum, stress, red, solid, spread):
    row_count, flat_count = density.shape
    sources = [density] + [momentum.at[axis] for axis in range(3)]
    sources = sources + [stress.at[part] for part in range(6)] + [red, solid]
    for index, source in enumerate(sources):
        for row in range(0, row_count, SUBLANES):
            for tile in range(flat_count // LANES):
                values = source[pl.ds(row, SUBLANES), pl.ds(tile * LANES, LANES)]
                start = row * SUBLANES + 1 + tile
                spread[index, pl.ds(start, SUBLANES, stride=SUBLANES), :] = values.astype(jnp.float32)


def spread_rows(arrays):
    row_count = arrays[0].shape[0]
    return pl.pallas_call(
        spread_kernel,
        out_shape=jax.ShapeDtypeStruct((PLANES, row_count * SUBLANES, LANES), jnp.float32),
        in_specs=[VMEM] * 5,
        out_specs=VMEM,
        compiler_params=pltpu.CompilerParams(vmem_limit_bytes=16 * 1024 * 1024),
        name="spread",
    )(*arrays)


def ends_kernel(info, spread, side, whole, low_end, high_end):
    live, low_part = info[0], info[3] == 0
    row_count = side.shape[1]
    for index in range(PLANES):
        whole[index] = spread[index]
        for row in range(0, row_count, SUBLANES):
            values = side[index, pl.ds(row, SUBLANES), :]
            start = row * SUBLANES
            below = jnp.where(low_part, 0.0, values)
            above = jnp.where(low_part, values, 0.0)
            whole[index, pl.ds(start, SUBLANES, stride=SUBLANES), :] = below
            whole[index, pl.ds(start + SUBLANES - 1, SUBLANES, stride=SUBLANES), :] = above
    for index in range(PLANES):
        target = pl.ds((1 + FULL * index) * SUBLANES, FULL * SUBLANES)
        low_end[target, :] = whole[index, pl.ds(0, FULL * SUBLANES), :]
        high_end[target, :] = whole[index, flat_rows(live - FULL, FULL), :]
    for end, row in ((low_end, FULL), (high_end, live - HALO)):
        rows = flat_rows(row, 1)
        end[pl.ds(0, SUBLANES), :] = 2.0 * whole[10, rows, :] - whole[0, rows, :]


def take_ends(info, spread, side):
    end = jax.ShapeDtypeStruct(((1 + FULL * PLANES) * SUBLANES, LANES), jnp.float32)
    return pl.pallas_call(
        ends_kernel,
        out_shape=[jax.ShapeDtypeStruct(spread.shape, jnp.float32), end, end],
        in_specs=[SMEM, VMEM, VMEM],
        out_specs=[VMEM] * 3,
        compiler_params=pltpu.CompilerParams(vmem_limit_bytes=16 * 1024 * 1024),
        name="ends",
    )(info, spread, side)


def inner_kernel(
    info, whole,
    density_out, momentum_out, stress_out, red_out, moved_rim, fields_rim, final_rim,
    colours, walls, moved, reds, fields, moved_later, reds_later, final,
):
    row_count, flat_count = density_out.shape
    own_tiles = flat_count // LANES
    geometry = Geometry(info, own_tiles)
    live = geometry.live
    fill_wall_table(walls, geometry)

    def colour(source, first, end):
        over_rows(geometry, first, end, COLOUR_BLOCK, lambda block: colour_stage(
            block, geometry, source, colours))

    def collide(source, target, target_reds, first, end):
        over_rows(geometry, first, end, COLLIDE_BLOCK, lambda block: collide_stage(
            block, geometry, source, whole, colours, walls, target, target_reds))

    def arrive(source, source_reds, target, first, end):
        over_rows(geometry, first, end, ARRIVE_BLOCK, lambda block: arrive_stage(
            block, geometry, walls, source, source_reds, target))

    colour(whole, 0, live)
    collide(whole, moved, reds, 1, live - 1)
    arrive(moved, reds, fields, 2, live - 2)
    colour(fields, 2, live - 2)
    collide(fields, moved_later, reds_later, 3, live - 3)
    arrive(moved_later, reds_later, final, 4, live - 4)

    def keep(target, target_index, source, index, rows, size):
        for place, row in enumerate(rows):
            target[target_index, flat_rows(place * size, size), :] = source[
                index, flat_rows(row, size), :
            ]

    for index in range(MOVED + REDS):
        first, later, at = moved, moved_later, index
        if index >= MOVED:
            first, later, at = reds, reds_later, index - MOVED
        keep(moved_rim, index, first, at, (1, live - 3), 2)
        keep(moved_rim, MOVED + REDS + index, later, at, (3, live - 5), 2)
    for index in range(FIELDS):
        keep(fields_rim, index, fields, index, (2, live - 4), 2)
        keep(final_rim, index, final, index, (RIM, live - 2 * RIM), RIM)

    targets = [density_out] + [momentum_out.at[axis] for axis in range(3)]
    targets = targets + [stress_out.at[part] for part in range(6)] + [red_out]
    for index, target in enumerate(targets):
        for row in range(0, row_count, SUBLANES):
            alive = row < live
            for tile in range(own_tiles):
                start = row * SUBLANES + 1 + tile
                values = final[index, pl.ds(start, SUBLANES, stride=SUBLANES), :]
                target[pl.ds(row, SUBLANES), pl.ds(tile * LANES, LANES)] = jnp.where(
                    alive, values, 0.0
                )


def run_inner(info, whole, arrays):
    flat = whole.shape[1]
    rim = lambda count, rows: jax.ShapeDtypeStruct((count, rows * SUBLANES, LANES), jnp.float32)
    shapes = [jax.ShapeDtypeStruct(array.shape, jnp.float32) for array in arrays[:4]]
    shapes = shapes + [rim(2 * (MOVED + REDS), 4), rim(FIELDS, 4), rim(FIELDS, 2 * RIM)]
    return pl.pallas_call(
        inner_kernel,
        out_shape=shapes,
        in_specs=[SMEM, VMEM],
        out_specs=[VMEM] * len(shapes),
        scratch_shapes=[
            pltpu.VMEM((4, flat, LANES), jnp.float32),
            pltpu.VMEM((4, 3 * SUBLANES, LANES), jnp.float32),
            pltpu.VMEM((MOVED, flat, LANES), jnp.float32),
            pltpu.VMEM((REDS, flat, LANES), jnp.float32),
            pltpu.VMEM((FIELDS, flat, LANES), jnp.float32),
            pltpu.VMEM((MOVED, flat, LANES), jnp.float32),
            pltpu.VMEM((REDS, flat, LANES), jnp.float32),
            pltpu.VMEM((FIELDS, flat, LANES), jnp.float32),
        ],
        compiler_params=pltpu.CompilerParams(vmem_limit_bytes=32 * 1024 * 1024),
        cost_estimate=pl.CostEstimate(flops=40_000_000, bytes_accessed=8_000_000, transcendentals=0),
        name="inner",
    )(info, whole)


def outer_kernel(
    info, whole, low, high, moved_rim, fields_rim, final_rim, *refs,
):
    outs = refs[4:8]
    start_fields, colours, walls, moved, reds, fields, moved_later, reds_later, final = refs[8:17]
    pieces, sems = refs[17:]
    row_count, flat_count = outs[0].shape
    own_tiles = flat_count // LANES
    geometry = Geometry(info, own_tiles)
    live = geometry.live
    fill_wall_table(walls, geometry)

    def spans(first, count):
        mirrored = SLAB - first - count
        return [
            (first - HALO, first, count),
            (live - 2 * RIM + mirrored, SLAB + mirrored, count),
        ]

    for index in range(PLANES):
        place = pl.ds((1 + FULL * index) * SUBLANES, FULL * SUBLANES)
        start_fields[index, flat_rows(1, FULL), :] = low[place, :]
        start_fields[index, flat_rows(2 * SLAB - HALO, FULL), :] = high[place, :]
        start_fields[index, flat_rows(HALO, 2), :] = whole[index, flat_rows(0, 2), :]
        start_fields[index, flat_rows(2 * SLAB - HALO - 2, 2), :] = whole[
            index, flat_rows(live - 2, 2), :
        ]
    for row, end in ((0, low), (2 * SLAB - 1, high)):
        start_fields[0, flat_rows(row, 1), :] = jnp.zeros((SUBLANES, LANES), jnp.float32)
        start_fields[10, flat_rows(row, 1), :] = 0.5 * end[pl.ds(0, SUBLANES), :]

    def place(target, index, source, at, first, size):
        for place, (row, local, count) in enumerate(spans(first, size)):
            target[index, flat_rows(local, size), :] = source[at, flat_rows(place * size, size), :]

    for index in range(MOVED + REDS):
        target, later, at = moved, moved_later, index
        if index >= MOVED:
            target, later, at = reds, reds_later, index - MOVED
        place(target, at, moved_rim, index, HALO + 1, 2)
        place(later, at, moved_rim, MOVED + REDS + index, HALO + 3, 2)
    for index in range(FIELDS):
        place(fields, index, fields_rim, index, HALO + 2, 2)
        place(final, index, final_rim, index, HALO + RIM, RIM)

    block = lambda first, count: Block(geometry, spans(first, count))
    colour_stage(block(0, 6), geometry, start_fields, colours)
    collide_stage(block(1, 4), geometry, start_fields, start_fields, colours, walls, moved, reds)
    arrive_stage(block(2, 4), geometry, walls, moved, reds, fields)
    start_fields[PLANES - 1, flat_rows(HALO + 2, 1), :] = whole[PLANES - 1, flat_rows(2, 1), :]
    start_fields[PLANES - 1, flat_rows(2 * SLAB - HALO - 3, 1), :] = whole[
        PLANES - 1, flat_rows(live - 3, 1), :
    ]
    colour_stage(block(2, 6), geometry, fields, colours)
    collide_stage(
        block(3, 4), geometry, fields, start_fields, colours, walls, moved_later, reds_later
    )
    arrive_stage(block(4, 4), geometry, walls, moved_later, reds_later, final)

    for index in range(FIELDS):
        for side, row in ((0, HALO), (1, SLAB)):
            for tile in range(own_tiles):
                start = row * SUBLANES + 1 + tile
                pieces[index, pl.ds(side * SUBLANES, SUBLANES), pl.ds(tile * LANES, LANES)] = final[
                    index, pl.ds(start, SUBLANES, stride=SUBLANES), :
                ]
    copies = []
    for side, row in ((0, 0), (1, pl.multiple_of(live - SUBLANES, SUBLANES))):
        rows = pl.ds(row, SUBLANES)
        held = pl.ds(side * SUBLANES, SUBLANES)
        for number, (out, source) in enumerate(
            (
                (outs[0].at[rows], pieces.at[0, held]),
                (outs[1].at[:, rows], pieces.at[pl.ds(1, 3), held]),
                (outs[2].at[:, rows], pieces.at[pl.ds(4, 6), held]),
                (outs[3].at[rows], pieces.at[10, held]),
            )
        ):
            copies.append(pltpu.make_async_copy(source, out, sems.at[side, number]))
    for copy in copies:
        copy.start()
    for copy in copies:
        copy.wait()


def run_outer(info, whole, low, high, rims, outs):
    flat = 2 * SLAB * SUBLANES
    flat_count = outs[0].shape[1]
    return pl.pallas_call(
        outer_kernel,
        out_shape=[jax.ShapeDtypeStruct(out.shape, jnp.float32) for out in outs],
        in_specs=[SMEM] + [VMEM] * 6 + [ANY] * 4,
        out_specs=[ANY] * 4,
        scratch_shapes=[
            pltpu.VMEM((PLANES, flat, LANES), jnp.float32),
            pltpu.VMEM((4, flat, LANES), jnp.float32),
            pltpu.VMEM((4, 3 * SUBLANES, LANES), jnp.float32),
            pltpu.VMEM((MOVED, flat, LANES), jnp.float32),
            pltpu.VMEM((REDS, flat, LANES), jnp.float32),
            pltpu.VMEM((FIELDS, flat, LANES), jnp.float32),
            pltpu.VMEM((MOVED, flat, LANES), jnp.float32),
            pltpu.VMEM((REDS, flat, LANES), jnp.float32),
            pltpu.VMEM((FIELDS, flat, LANES), jnp.float32),
            pltpu.VMEM((FIELDS, 2 * SUBLANES, flat_count), jnp.float32),
            pltpu.SemaphoreType.DMA((2, 4)),
        ],
        input_output_aliases={7: 0, 8: 1, 9: 2, 10: 3},
        compiler_params=pltpu.CompilerParams(vmem_limit_bytes=32 * 1024 * 1024),
        name="outer",
    )(info, whole, low, high, *rims, *outs)


def body(density, momentum, stress, red_density, solid, widths):
    tiles_index = lax.axis_index("tiles")
    tiles_count = lax.axis_size("tiles")
    chosen = lax.iota(jnp.int32, widths.shape[0]) == tiles_index
    live_rows = jnp.sum(jnp.where(chosen, widths, 0)) * TILE
    info = jnp.stack(
        [
            live_rows,
            (tiles_index == 0).astype(jnp.int32),
            (tiles_index == tiles_count - 1).astype(jnp.int32),
            lax.axis_index("sub").astype(jnp.int32),
        ]
    )
    arrays = (density, momentum, stress, red_density, solid)
    side = lax.ppermute(take_edge(arrays), "sub", [(0, 1), (1, 0)])
    whole, low_end, high_end = take_ends(info, spread_rows(arrays), side)
    ends = tiles_count - 1
    low = lax.ppermute(high_end, "tiles", [(i, i + 1) for i in range(ends)])
    high = lax.ppermute(low_end, "tiles", [(i + 1, i) for i in range(ends)])
    results = run_inner(info, whole, arrays)
    return tuple(run_outer(info, whole, low, high, results[4:], results[:4]))


def solution(mesh):
    in_specs = (
        P(("groups", "tiles"), "sub"),
        P(None, ("groups", "tiles"), "sub"),
        P(None, ("groups", "tiles"), "sub"),
        P(("groups", "tiles"), "sub"),
        P(("groups", "tiles"), "sub"),
        P("groups"),
    )
    out_specs = (
        P(("groups", "tiles"), "sub"),
        P(None, ("groups", "tiles"), "sub"),
        P(None, ("groups", "tiles"), "sub"),
        P(("groups", "tiles"), "sub"),
    )
    return jax.shard_map(body, mesh=mesh, in_specs=in_specs, out_specs=out_specs, check_vma=False)
```

time: 42.9 us -> 29.7 us (0.69)
  the two profiles are of different devices: /device:TPU:27 before, /device:TPU:19 now
where the time goes in v2:
time: 29.7 us; the launch traced here: 29.5 us
  Pallas kernels  16.6 us (56%)
  starting transfers between devices  6.92 us (23%)
  local copies, waits for them, and re-layouts  3.75 us (13%)
  between operations  1.39 us (5%)
  other arithmetic  0.78 us (3%)
    pallas_call x1, Pallas kernels, run_inner(): pl.pallas_call(inner_kernel, out_shape=shapes, in_specs=[SMEM, VMEM], out...  11 us
    unnamed x12, local copies, waits for them, and re-layouts  3.75 us
    ppermute x1, starting transfers between devices, body(): low = lax.ppermute(high_end, 'tiles', [(i, i + 1) for i in range(ends)])  3.15 us
    ppermute x1, starting transfers between devices, body(): high = lax.ppermute(low_end, 'tiles', [(i + 1, i) for i in range(ends)])  3.03 us
    pallas_call x1, Pallas kernels, run_outer(): pl.pallas_call(outer_kernel, out_shape=[jax.ShapeDtypeStruct(out.shape, j...  2.72 us
    pallas_call x1, Pallas kernels, take_edge(): pl.pallas_call(edge_kernel, out_shape=jax.ShapeDtypeStruct((PLANES, row_c...  1.81 us
    pallas_call x1, Pallas kernels, take_ends(): pl.pallas_call(ends_kernel, out_shape=[jax.ShapeDtypeStruct(spread.shape,...  0.81 us
    ppermute x1, starting transfers between devices, body(): side = lax.ppermute(take_edge(arrays), 'sub', [(0, 1), (1, 0)])  0.74 us
  transfers between devices with their start and end apart: 3, of which 0 were waited for; matrix products, arithmetic and copies ran while one was open for 3% of the time, Pallas kernels for 38%

profile of v2, /device:TPU:19, one launch (start us, length us, event | category | flops | bytes accessed | tf_op | source)
XLA Modules:
  0.0 29.5 jit_solution(6807888220802093180)
XLA Ops:
  0.6 0.0 copy-start
  0.6 1.8 %edge.1 = f32[12,48,128]{2,1,0:T(8,128)} custom-call(f32[48,768]{1,0:T(8,128)} %density.3, f32[3,48,768]{2,1,0:T(8,128)} %momentum.3, f32[6,48,768]{2,1,0:T(8,128)} %stress.3, f32[48,768]{1,0:T(8,128)} %red.3, s32[48,768]{1,0:T(8,128)} %solid.3), custom_call_target="tpu_custom_call" | custom-call | tf_op jit(solution)/shard_map/edge/pallas_call | solution.py:357
  2.5 0.0 copy-start.5
  2.5 0.7 %collective-permute-start = (f32[12,48,128]{2,1,0:T(8,128)}, f32[12,48,128]{2,1,0:T(8,128)S(1)}, u32[]{:S(2)}, u32[]{:S(2)}) collective-permute-start(f32[12,48,128]{2,1,0:T(8,128)} %edge.1), channel_id=1, source_target_pairs={{0,1},{1,0},{2,3},{3,2},{4,5},{5,4},{6,7},{7,6},{8,9},{9,8},{10,11... | collective-permute-start | bytes 884744 | tf_op jit(solution)/shard_map/ppermute | solution.py:635
  3.2 0.0 copy-done
  3.2 0.0 copy-start.1
  3.2 1.0 %copy-done.1 = f32[3,48,768]{2,1,0:T(8,128)S(1)} copy-done((f32[3,48,768]{2,1,0:T(8,128)S(1)}, f32[3,48,768]{2,1,0:T(8,128)}, u32[]{:S(2)}) %copy-start.1) | copy-done | bytes 442392
  4.2 0.0 copy-start.2
  4.2 0.9 %copy-done.2 = f32[48,768]{1,0:T(8,128)S(1)} copy-done((f32[48,768]{1,0:T(8,128)S(1)}, f32[48,768]{1,0:T(8,128)}, u32[]{:S(2)}) %copy-start.2) | copy-done | bytes 147480
  5.1 0.0 copy-start.3
  5.1 0.9 %copy-done.3 = f32[48,768]{1,0:T(8,128)S(1)} copy-done((f32[48,768]{1,0:T(8,128)S(1)}, f32[48,768]{1,0:T(8,128)}, u32[]{:S(2)}) %copy-start.3) | copy-done | bytes 147480
  6.1 0.0 copy-start.4
  6.1 0.9 %copy-done.4 = s32[48,768]{1,0:T(8,128)S(1)} copy-done((s32[48,768]{1,0:T(8,128)S(1)}, s32[48,768]{1,0:T(8,128)}, u32[]{:S(2)}) %copy-start.4) | copy-done | bytes 147480
  7.0 0.3 %spread.1 = f32[12,384,128]{2,1,0:T(8,128)S(1)} custom-call(f32[48,768]{1,0:T(8,128)S(1)} %copy-done.2, f32[3,48,768]{2,1,0:T(8,128)S(1)} %copy-done.1, f32[6,48,768]{2,1,0:T(8,128)S(1)} %copy-done, f32[48,768]{1,0:T(8,128)S(1)} %copy-done.3, s32[48,768]{1,0:T(8,128)S(1)} %copy-done.4), custom_call_target="tpu_custom_call" | custom-call | tf_op jit(solution)/shard_map/spread/pallas_call | solution.py:381
  7.3 0.0 copy-done.5
  7.3 0.7 %fusion = s32[]{:T(128)} fusion(s32[8]{0:T(128)S(1)} %copy-done.5, s32[]{:T(128)S(6)} %axis_index.23), kind=kLoop, calls=%fused_computation.1 | loop fusion | flops 23 | bytes 40 | tf_op jit(solution)/shard_map/reduce_sum | solution.py:625
  8.7 0.1 pad_add_fusion.info
  8.8 0.0 collective-permute-done.side
  8.8 0.8 %ends.1 = (f32[12,384,128]{2,1,0:T(8,128)S(1)}, f32[296,128]{1,0:T(8,128)S(1)}, f32[296,128]{1,0:T(8,128)S(1)}) custom-call(s32[4]{0:T(128)S(1)} %pad_add_fusion.info, f32[12,384,128]{2,1,0:T(8,128)S(1)} %spread.1, f32[12,48,128]{2,1,0:T(8,128)S(1)} %collective-permute-done.side), custom_call_target="tpu_custom_call" | custom-call | tf_op jit(solution)/shard_map/ends/pallas_call | solution.py:414
  9.6 3.1 %collective-permute-start.1 = (f32[296,128]{1,0:T(8,128)S(1)}, f32[296,128]{1,0:T(8,128)S(1)}, u32[]{:S(2)}, u32[]{:S(2)}) collective-permute-start(f32[296,128]{1,0:T(8,128)S(1)} %get-tuple-element.15), channel_id=1, source_target_pairs={{0,2},{2,4},{4,6},{6,8},{8,10},{10,12},{12,14},{1,3},{3,5},{5,7},{... | collective-permute-start | bytes 454664 | tf_op jit(solution)/shard_map/ppermute | solution.py:638
  12.7 3.0 %collective-permute-start.2 = (f32[296,128]{1,0:T(8,128)S(1)}, f32[296,128]{1,0:T(8,128)S(1)}, u32[]{:S(2)}, u32[]{:S(2)}) collective-permute-start(f32[296,128]{1,0:T(8,128)S(1)} %get-tuple-element.16), channel_id=1, source_target_pairs={{2,0},{4,2},{6,4},{8,6},{10,8},{12,10},{14,12},{3,1},{5,3},{7,5},{... | collective-permute-start | bytes 454664 | tf_op jit(solution)/shard_map/ppermute | solution.py:639
  15.8 11.0 %inner.1 = (f32[48,768]{1,0:T(8,128)}, f32[3,48,768]{2,1,0:T(8,128)}, f32[6,48,768]{2,1,0:T(8,128)}, f32[48,768]{1,0:T(8,128)}, f32[48,32,128]{2,1,0:T(8,128)S(1...) custom-call(s32[4]{0:T(128)S(1)} %pad_add_fusion.info, f32[12,384,128]{2,1,0:T(8,128)S(1)} %get-tuple-element.14.whole), custom_call_target="tpu_custom_call" | custom-call | flops 40000000 | bytes 8000000 | tf_op jit(solution)/shard_map/inner/pallas_call | solution.py:488
  26.7 0.0 collective-permute-done.1.low
  26.7 0.0 collective-permute-done.2.high
  26.7 2.7 %outer.1 = (f32[48,768]{1,0:T(8,128)}, f32[3,48,768]{2,1,0:T(8,128)}, f32[6,48,768]{2,1,0:T(8,128)}, f32[48,768]{1,0:T(8,128)}) custom-call(s32[4]{0:T(128)S(1)} %pad_add_fusion.info, f32[12,384,128]{2,1,0:T(8,128)S(1)} %get-tuple-element.14.whole, ...), custom_call_target="tpu_custom_call", output_to_operand_aliasing={{0}: (7, {}), {1}: (8, {}), {2}: (9, {}), {3}: (10, {})} | custom-call | tf_op jit(solution)/shard_map/outer/pallas_call | solution.py:597
Async XLA Ops:
  0.6 2.6 %copy-start = (f32[6,48,768]{2,1,0:T(8,128)S(1)}, f32[6,48,768]{2,1,0:T(8,128)}, u32[]{:S(2)}) copy-start(f32[6,48,768]{2,1,0:T(8,128)} %stress.3) | copy-start | bytes 2654212
  2.5 4.8 %copy-start.5 = (s32[8]{0:T(128)S(1)}, s32[8]{0:T(128)}, u32[]{:S(2)}) copy-start(s32[8]{0:T(128)} %param.11) | copy-start | bytes 100
  2.5 6.3 %collective-permute-start = (f32[12,48,128]{2,1,0:T(8,128)}, f32[12,48,128]{2,1,0:T(8,128)S(1)}, u32[]{:S(2)}, u32[]{:S(2)}) collective-permute-start(f32[12,48,128]{2,1,0:T(8,128)} %edge.1), channel_id=1, source_target_pairs={{0,1},{1,0},{2,3},{3,2},{4,5},{5,4},{6,7},{7,6},{8,9},{9,8},{10,11... | collective-permute-start | bytes 884744 | tf_op jit(solution)/shard_map/ppermute | solution.py:635
  3.2 1.0 %copy-start.1 = (f32[3,48,768]{2,1,0:T(8,128)S(1)}, f32[3,48,768]{2,1,0:T(8,128)}, u32[]{:S(2)}) copy-start(f32[3,48,768]{2,1,0:T(8,128)} %momentum.3) | copy-start | bytes 1327108
  4.2 0.9 %copy-start.2 = (f32[48,768]{1,0:T(8,128)S(1)}, f32[48,768]{1,0:T(8,128)}, u32[]{:S(2)}) copy-start(f32[48,768]{1,0:T(8,128)} %density.3) | copy-start | bytes 442372
  5.1 0.9 %copy-start.3 = (f32[48,768]{1,0:T(8,128)S(1)}, f32[48,768]{1,0:T(8,128)}, u32[]{:S(2)}) copy-start(f32[48,768]{1,0:T(8,128)} %red.3) | copy-start | bytes 442372
  6.1 0.9 %copy-start.4 = (s32[48,768]{1,0:T(8,128)S(1)}, s32[48,768]{1,0:T(8,128)}, u32[]{:S(2)}) copy-start(s32[48,768]{1,0:T(8,128)} %solid.3) | copy-start | bytes 442372
  9.6 17.2 %collective-permute-start.1 = (f32[296,128]{1,0:T(8,128)S(1)}, f32[296,128]{1,0:T(8,128)S(1)}, u32[]{:S(2)}, u32[]{:S(2)}) collective-permute-start(f32[296,128]{1,0:T(8,128)S(1)} %get-tuple-element.15), channel_id=1, source_target_pairs={{0,2},{2,4},{4,6},{6,8},{8,10},{10,12},{12,14},{1,3},{3,5},{5,7},{... | collective-permute-start | bytes 454664 | tf_op jit(solution)/shard_map/ppermute | solution.py:638
  12.7 14.0 %collective-permute-start.2 = (f32[296,128]{1,0:T(8,128)S(1)}, f32[296,128]{1,0:T(8,128)S(1)}, u32[]{:S(2)}, u32[]{:S(2)}) collective-permute-start(f32[296,128]{1,0:T(8,128)S(1)} %get-tuple-element.16), channel_id=1, source_target_pairs={{2,0},{4,2},{6,4},{8,6},{10,8},{12,10},{14,12},{3,1},{5,3},{7,5},{... | collective-permute-start | bytes 454664 | tf_op jit(solution)/shard_map/ppermute | solution.py:639

commit v3 on v2

--- a/solution.py
+++ b/solution.py
@@ -23,9 +23,11 @@
 REDS = 5
 RIM = 4
 SLAB = HALO + 2 * RIM
-COLOUR_BLOCK = 8
-COLLIDE_BLOCK = 4
-ARRIVE_BLOCK = 4
+END_ROWS = (1 + FULL * PLANES) * SUBLANES
+OWN_TILES = SUBLANES - 2
+COLOUR_BLOCK = (8, 1)
+COLLIDE_BLOCK = (4, 2)
+ARRIVE_BLOCK = (4, 2)
 VMEM = pl.BlockSpec(memory_space=pltpu.VMEM)
 SMEM = pl.BlockSpec(memory_space=pltpu.SMEM)
 ANY = pl.BlockSpec(memory_space=pl.ANY)
@@ -325,154 +327,182 @@
     block.store(fields, 10, red_total)
 
 
-def over_rows(geometry, first, end, size, stage):
+def over_rows(geometry, first, end, size, blocks, stage):
+    trip = size * blocks
+
     def step(index, carry):
-        row = jnp.minimum(first + index * size, end - size)
-        stage(Block(geometry, [(row, row, size)], inner=True))
+        start = jnp.minimum(first + index * trip, end - trip)
+        for number in range(blocks):
+            row = start + number * size
+            stage(Block(geometry, [(row, row, size)], inner=True))
         return carry
 
-    lax.fori_loop(0, (end - first + size - 1) // size, step, 0)
-
-
-def edge_kernel(density, momentum, stress, red, solid, edge, solid_edge, sems):
-    own_tiles = density.shape[1] // LANES
-    start = jnp.where(lax.axis_index("sub") == 0, (own_tiles - 1) * LANES, 0)
-    lanes = pl.ds(pl.multiple_of(start, LANES), LANES)
+    lax.fori_loop(0, (end - first + trip - 1) // trip, step, 0)
+
+
+def load_kernel(
+    tiles_count, density, momentum, stress, red, solid, widths,
+    info, spread, packet, mine,
+    raw, raw_solid, held_widths, sems,
+):
+    row_count, flat_count = raw_solid.shape
+    own_tiles = flat_count // LANES
     copies = [
-        pltpu.make_async_copy(density.at[:, lanes], edge.at[0], sems.at[0]),
-        pltpu.make_async_copy(momentum.at[:, :, lanes], edge.at[pl.ds(1, 3)], sems.at[1]),
-        pltpu.make_async_copy(stress.at[:, :, lanes], edge.at[pl.ds(4, 6)], sems.at[2]),
-        pltpu.make_async_copy(red.at[:, lanes], edge.at[10], sems.at[3]),
-        pltpu.make_async_copy(solid.at[:, lanes], solid_edge, sems.at[4]),
+        pltpu.make_async_copy(widths, held_widths, sems.at[0]),
+        pltpu.make_async_copy(density, raw.at[0], sems.at[1]),
+        pltpu.make_async_copy(momentum, raw.at[pl.ds(1, 3)], sems.at[2]),
+        pltpu.make_async_copy(stress, raw.at[pl.ds(4, 6)], sems.at[3]),
+        pltpu.make_async_copy(red, raw.at[10], sems.at[4]),
+        pltpu.make_async_copy(solid, raw_solid, sems.at[5]),
     ]
     for copy in copies:
         copy.start()
-    for copy in copies:
-        copy.wait()
-    edge[PLANES - 1] = solid_edge[...].astype(jnp.float32)
-
-
-def take_edge(arrays):
-    row_count = arrays[0].shape[0]
+    tiles_index, sub_index = lax.axis_index("tiles"), lax.axis_index("sub")
+    low_part = sub_index == 0
+    edge_start = pl.multiple_of(jnp.where(low_part, (own_tiles - 1) * LANES, 0), LANES)
+
+    copies[0].wait()
+    live = held_widths[tiles_index] * TILE
+    info[0] = live
+    info[1] = (tiles_index == 0).astype(jnp.int32)
+    info[2] = (tiles_index == tiles_count - 1).astype(jnp.int32)
+    info[3] = sub_index
+
+    ready = {0: copies[1], 1: copies[2], 4: copies[3], 10: copies[4], 11: copies[5]}
+    for index in range(PLANES):
+        if index in ready:
+            ready[index].wait()
+        source = raw_solid if index == FIELDS else raw.at[index]
+        for row in range(0, row_count, SUBLANES):
+            rows = pl.ds(row, SUBLANES)
+            for tile in range(own_tiles):
+                values = source[rows, pl.ds(tile * LANES, LANES)].astype(jnp.float32)
+                start = row * SUBLANES + 1 + tile
+                spread[index, pl.ds(start, SUBLANES, stride=SUBLANES), :] = values
+            values = source[rows, pl.ds(edge_start, LANES)].astype(jnp.float32)
+            packet[pl.ds(index * row_count + row, SUBLANES), :] = values
+
+    after = PLANES * row_count
+    ends = (
+        (packet, after, jnp.where(low_part, 0, live - FULL), jnp.where(low_part, FULL, live - HALO)),
+        (mine, 0, jnp.where(low_part, live - FULL, 0), jnp.where(low_part, live - HALO, FULL)),
+    )
+    for target, at, full_row, colour_row in ends:
+        rows = flat_rows(colour_row, 1)
+        target[pl.ds(at, SUBLANES), :] = 2.0 * spread[10, rows, :] - spread[0, rows, :]
+        for index in range(PLANES):
+            place = pl.ds(at + (1 + FULL * index) * SUBLANES, FULL * SUBLANES)
+            target[place, :] = spread[index, flat_rows(full_row, FULL), :]
+
+
+def load_inputs(arrays, widths, tiles_count):
+    row_count, flat_count = arrays[0].shape
+    packet_rows = PLANES * row_count + END_ROWS
     return pl.pallas_call(
-        edge_kernel,
-        out_shape=jax.ShapeDtypeStruct((PLANES, row_count, LANES), jnp.float32),
-        in_specs=[HBM] * 5,
-        out_specs=VMEM,
-        scratch_shapes=[pltpu.VMEM((row_count, LANES), jnp.int32), pltpu.SemaphoreType.DMA((5,))],
-        name="edge",
-    )(*arrays)
-
-
-def spread_kernel(density, momentum, stress, red, solid, spread):
-    row_count, flat_count = density.shape
-    sources = [density] + [momentum.at[axis] for axis in range(3)]
-    sources = sources + [stress.at[part] for part in range(6)] + [red, solid]
-    for index, source in enumerate(sources):
-        for row in range(0, row_count, SUBLANES):
-            for tile in range(flat_count // LANES):
-                values = source[pl.ds(row, SUBLANES), pl.ds(tile * LANES, LANES)]
-                start = row * SUBLANES + 1 + tile
-                spread[index, pl.ds(start, SUBLANES, stride=SUBLANES), :] = values.astype(jnp.float32)
-
-
-def spread_rows(arrays):
-    row_count = arrays[0].shape[0]
-    return pl.pallas_call(
-        spread_kernel,
-        out_shape=jax.ShapeDtypeStruct((PLANES, row_count * SUBLANES, LANES), jnp.float32),
-        in_specs=[VMEM] * 5,
-        out_specs=VMEM,
+        functools.partial(load_kernel, tiles_count),
+        out_shape=[
+            jax.ShapeDtypeStruct((4,), jnp.int32),
+            jax.ShapeDtypeStruct((PLANES, row_count * SUBLANES, LANES), jnp.float32),
+            jax.ShapeDtypeStruct((packet_rows, LANES), jnp.float32),
+            jax.ShapeDtypeStruct((END_ROWS, LANES), jnp.float32),
+        ],
+        in_specs=[HBM] * 6,
+        out_specs=[SMEM, VMEM, VMEM, VMEM],
+        scratch_shapes=[
+            pltpu.VMEM((FIELDS, row_count, flat_count), jnp.float32),
+            pltpu.VMEM((row_count, flat_count), jnp.int32),
+            pltpu.SMEM(widths.shape, jnp.int32),
+            pltpu.SemaphoreType.DMA((6,)),
+        ],
         compiler_params=pltpu.CompilerParams(vmem_limit_bytes=16 * 1024 * 1024),
-        name="spread",
-    )(*arrays)
-
-
-def ends_kernel(info, spread, side, whole, low_end, high_end):
-    live, low_part = info[0], info[3] == 0
-    row_count = side.shape[1]
+        name="load",
+    )(*arrays, widths)
+
+
+def join_kernel(info, spread, packet, mine, whole, ends):
+    low_part = info[3] == 0
+    row_count = spread.shape[1] // SUBLANES
+    ends[pl.ds(0, END_ROWS), :] = mine[...]
+    ends[pl.ds(END_ROWS, END_ROWS), :] = packet[pl.ds(PLANES * row_count, END_ROWS), :]
     for index in range(PLANES):
         whole[index] = spread[index]
         for row in range(0, row_count, SUBLANES):
-            values = side[index, pl.ds(row, SUBLANES), :]
+            values = packet[pl.ds(index * row_count + row, SUBLANES), :]
             start = row * SUBLANES
             below = jnp.where(low_part, 0.0, values)
             above = jnp.where(low_part, values, 0.0)
             whole[index, pl.ds(start, SUBLANES, stride=SUBLANES), :] = below
             whole[index, pl.ds(start + SUBLANES - 1, SUBLANES, stride=SUBLANES), :] = above
-    for index in range(PLANES):
-        target = pl.ds((1 + FULL * index) * SUBLANES, FULL * SUBLANES)
-        low_end[target, :] = whole[index, pl.ds(0, FULL * SUBLANES), :]
-        high_end[target, :] = whole[index, flat_rows(live - FULL, FULL), :]
-    for end, row in ((low_end, FULL), (high_end, live - HALO)):
-        rows = flat_rows(row, 1)
-        end[pl.ds(0, SUBLANES), :] = 2.0 * whole[10, rows, :] - whole[0, rows, :]
-
-
-def take_ends(info, spread, side):
-    end = jax.ShapeDtypeStruct(((1 + FULL * PLANES) * SUBLANES, LANES), jnp.float32)
+
+
+def join_parts(info, spread, packet, mine):
     return pl.pallas_call(
-        ends_kernel,
-        out_shape=[jax.ShapeDtypeStruct(spread.shape, jnp.float32), end, end],
-        in_specs=[SMEM, VMEM, VMEM],
-        out_specs=[VMEM] * 3,
+        join_kernel,
+        out_shape=[
+            jax.ShapeDtypeStruct(spread.shape, jnp.float32),
+            jax.ShapeDtypeStruct((2 * END_ROWS, LANES), jnp.float32),
+        ],
+        in_specs=[SMEM, VMEM, VMEM, VMEM],
+        out_specs=[VMEM] * 2,
         compiler_params=pltpu.CompilerParams(vmem_limit_bytes=16 * 1024 * 1024),
-        name="ends",
-    )(info, spread, side)
-
-
-def inner_kernel(
-    info, whole,
-    density_out, momentum_out, stress_out, red_out, moved_rim, fields_rim, final_rim,
-    colours, walls, moved, reds, fields, moved_later, reds_later, final,
+        name="join",
+    )(info, spread, packet, mine)
+
+
+def keep_rows(target, target_index, source, index, rows, size):
+    for place, row in enumerate(rows):
+        target[target_index, flat_rows(place * size, size), :] = source[
+            index, flat_rows(row, size), :
+        ]
+
+
+def inner_step(geometry, before, whole, first, scratch, after):
+    colours, walls, moved, reds = scratch
+    end = geometry.live - first
+    over_rows(geometry, first, end, *COLOUR_BLOCK, lambda block: colour_stage(
+        block, geometry, before, colours))
+    over_rows(geometry, first + 1, end - 1, *COLLIDE_BLOCK, lambda block: collide_stage(
+        block, geometry, before, whole, colours, walls, moved, reds))
+    over_rows(geometry, first + 2, end - 2, *ARRIVE_BLOCK, lambda block: arrive_stage(
+        block, geometry, walls, moved, reds, after))
+
+
+def keep_moved(target, moved, reds, rows):
+    for index in range(MOVED):
+        keep_rows(target, index, moved, index, rows, 2)
+    for index in range(REDS):
+        keep_rows(target, MOVED + index, reds, index, rows, 2)
+
+
+def first_kernel(info, whole, fields, moved_rim, fields_rim, *scratch):
+    geometry = Geometry(info, OWN_TILES)
+    live = geometry.live
+    fill_wall_table(scratch[1], geometry)
+    inner_step(geometry, whole, whole, 0, scratch, fields)
+    keep_moved(moved_rim, scratch[2], scratch[3], (1, live - 3))
+    for index in range(FIELDS):
+        keep_rows(fields_rim, index, fields, index, (2, live - 4), 2)
+
+
+def second_kernel(
+    info, whole, fields, arrived, density_out, momentum_out, stress_out, red_out,
+    moved_rim, final_rim, final, *scratch,
 ):
     row_count, flat_count = density_out.shape
-    own_tiles = flat_count // LANES
-    geometry = Geometry(info, own_tiles)
+    geometry = Geometry(info, OWN_TILES)
     live = geometry.live
-    fill_wall_table(walls, geometry)
-
-    def colour(source, first, end):
-        over_rows(geometry, first, end, COLOUR_BLOCK, lambda block: colour_stage(
-            block, geometry, source, colours))
-
-    def collide(source, target, target_reds, first, end):
-        over_rows(geometry, first, end, COLLIDE_BLOCK, lambda block: collide_stage(
-            block, geometry, source, whole, colours, walls, target, target_reds))
-
-    def arrive(source, source_reds, target, first, end):
-        over_rows(geometry, first, end, ARRIVE_BLOCK, lambda block: arrive_stage(
-            block, geometry, walls, source, source_reds, target))
-
-    colour(whole, 0, live)
-    collide(whole, moved, reds, 1, live - 1)
-    arrive(moved, reds, fields, 2, live - 2)
-    colour(fields, 2, live - 2)
-    collide(fields, moved_later, reds_later, 3, live - 3)
-    arrive(moved_later, reds_later, final, 4, live - 4)
-
-    def keep(target, target_index, source, index, rows, size):
-        for place, row in enumerate(rows):
-            target[target_index, flat_rows(place * size, size), :] = source[
-                index, flat_rows(row, size), :
-            ]
-
-    for index in range(MOVED + REDS):
-        first, later, at = moved, moved_later, index
-        if index >= MOVED:
-            first, later, at = reds, reds_later, index - MOVED
-        keep(moved_rim, index, first, at, (1, live - 3), 2)
-        keep(moved_rim, MOVED + REDS + index, later, at, (3, live - 5), 2)
+    fill_wall_table(scratch[1], geometry)
+    inner_step(geometry, fields, whole, 2, scratch, final)
+    keep_moved(moved_rim, scratch[2], scratch[3], (3, live - 5))
     for index in range(FIELDS):
-        keep(fields_rim, index, fields, index, (2, live - 4), 2)
-        keep(final_rim, index, final, index, (RIM, live - 2 * RIM), RIM)
+        keep_rows(final_rim, index, final, index, (RIM, live - 2 * RIM), RIM)
 
     targets = [density_out] + [momentum_out.at[axis] for axis in range(3)]
     targets = targets + [stress_out.at[part] for part in range(6)] + [red_out]
     for index, target in enumerate(targets):
         for row in range(0, row_count, SUBLANES):
             alive = row < live
-            for tile in range(own_tiles):
+            for tile in range(OWN_TILES):
                 start = row * SUBLANES + 1 + tile
                 values = final[index, pl.ds(start, SUBLANES, stride=SUBLANES), :]
                 target[pl.ds(row, SUBLANES), pl.ds(tile * LANES, LANES)] = jnp.where(
@@ -480,43 +510,99 @@
                 )
 
 
-def run_inner(info, whole, arrays):
+def inner_scratch(flat):
+    return [
+        pltpu.VMEM((4, flat, LANES), jnp.float32),
+        pltpu.VMEM((4, 3 * SUBLANES, LANES), jnp.float32),
+        pltpu.VMEM((MOVED, flat, LANES), jnp.float32),
+        pltpu.VMEM((REDS, flat, LANES), jnp.float32),
+    ]
+
+
+def rim_shape(count, rows):
+    return jax.ShapeDtypeStruct((count, rows * SUBLANES, LANES), jnp.float32)
+
+
+def run_first(info, whole):
     flat = whole.shape[1]
-    rim = lambda count, rows: jax.ShapeDtypeStruct((count, rows * SUBLANES, LANES), jnp.float32)
-    shapes = [jax.ShapeDtypeStruct(array.shape, jnp.float32) for array in arrays[:4]]
-    shapes = shapes + [rim(2 * (MOVED + REDS), 4), rim(FIELDS, 4), rim(FIELDS, 2 * RIM)]
+    shapes = [
+        jax.ShapeDtypeStruct((FIELDS, flat, LANES), jnp.float32),
+        rim_shape(MOVED + REDS, 4),
+        rim_shape(FIELDS, 4),
+    ]
     return pl.pallas_call(
-        inner_kernel,
+        first_kernel,
         out_shape=shapes,
         in_specs=[SMEM, VMEM],
         out_specs=[VMEM] * len(shapes),
-        scratch_shapes=[
-            pltpu.VMEM((4, flat, LANES), jnp.float32),
-            pltpu.VMEM((4, 3 * SUBLANES, LANES), jnp.float32),
-            pltpu.VMEM((MOVED, flat, LANES), jnp.float32),
-            pltpu.VMEM((REDS, flat, LANES), jnp.float32),
-            pltpu.VMEM((FIELDS, flat, LANES), jnp.float32),
-            pltpu.VMEM((MOVED, flat, LANES), jnp.float32),
-            pltpu.VMEM((REDS, flat, LANES), jnp.float32),
-            pltpu.VMEM((FIELDS, flat, LANES), jnp.float32),
-        ],
-        compiler_params=pltpu.CompilerParams(vmem_limit_bytes=32 * 1024 * 1024),
-        cost_estimate=pl.CostEstimate(flops=40_000_000, bytes_accessed=8_000_000, transcendentals=0),
-        name="inner",
+        scratch_shapes=inner_scratch(flat),
+        compiler_params=pltpu.CompilerParams(vmem_limit_bytes=24 * 1024 * 1024),
+        cost_estimate=pl.CostEstimate(flops=20_000_000, bytes_accessed=8_000_000, transcendentals=0),
+        name="first",
     )(info, whole)
 
 
+def run_second(info, whole, fields, arrived, arrays):
+    flat = whole.shape[1]
+    shapes = [jax.ShapeDtypeStruct(array.shape, jnp.float32) for array in arrays[:4]]
+    shapes = shapes + [rim_shape(MOVED + REDS, 4), rim_shape(FIELDS, 2 * RIM)]
+    return pl.pallas_call(
+        second_kernel,
+        out_shape=shapes,
+        in_specs=[SMEM, VMEM, VMEM, ANY],
+        out_specs=[VMEM] * len(shapes),
+        scratch_shapes=[pltpu.VMEM((FIELDS, flat, LANES), jnp.float32)] + inner_scratch(flat),
+        compiler_params=pltpu.CompilerParams(vmem_limit_bytes=24 * 1024 * 1024),
+        cost_estimate=pl.CostEstimate(flops=20_000_000, bytes_accessed=8_000_000, transcendentals=0),
+        name="second",
+    )(info, whole, fields, arrived)
+
+
+def turn_kernel(info, ends, kept, own, passing):
+    low_part = info[3] == 0
+    count = END_ROWS // SUBLANES
+    first = ends[pl.ds(0, END_ROWS), :].reshape(count, SUBLANES, LANES)
+    second = ends[pl.ds(END_ROWS, END_ROWS), :].reshape(count, SUBLANES, LANES)
+    tile = lax.broadcasted_iota(jnp.int32, (1, SUBLANES, LANES), 1)
+    middle = (tile >= 1) & (tile <= OWN_TILES)
+
+    def widened(part, other, low):
+        above = jnp.where(tile == 0, 0.0, pltpu.roll(other, OWN_TILES, 1))
+        below = jnp.where(tile == 0, pltpu.roll(other, SUBLANES - OWN_TILES, 1), 0.0)
+        full = jnp.where(middle, part, jnp.where(low, above, below))
+        return full.reshape(END_ROWS, LANES)
+
+    own[...] = widened(first, second, low_part)
+    passing[...] = widened(second, first, jnp.logical_not(low_part))
+
+
+def turn_ends(info, ends, kept):
+    shape = jax.ShapeDtypeStruct((END_ROWS, LANES), jnp.float32)
+    return pl.pallas_call(
+        turn_kernel,
+        out_shape=[shape, shape],
+        in_specs=[SMEM, VMEM, ANY],
+        out_specs=[VMEM] * 2,
+        compiler_params=pltpu.CompilerParams(vmem_limit_bytes=8 * 1024 * 1024),
+        name="turn",
+    )(info, ends, kept)
+
+
 def outer_kernel(
-    info, whole, low, high, moved_rim, fields_rim, final_rim, *refs,
+    info, whole, arrived, passed, moved_rim, fields_rim, moved_later_rim, final_rim, *refs,
 ):
     outs = refs[4:8]
     start_fields, colours, walls, moved, reds, fields, moved_later, reds_later, final = refs[8:17]
     pieces, sems = refs[17:]
-    row_count, flat_count = outs[0].shape
-    own_tiles = flat_count // LANES
-    geometry = Geometry(info, own_tiles)
+    geometry = Geometry(info, OWN_TILES)
     live = geometry.live
+    low_part = info[3] == 0
     fill_wall_table(walls, geometry)
+
+    def received(place, count):
+        rows = pl.ds(place, count * SUBLANES)
+        straight, crossed = arrived[rows, :], passed[rows, :]
+        return jnp.where(low_part, straight, crossed), jnp.where(low_part, crossed, straight)
 
     def spans(first, count):
         mirrored = SLAB - first - count
@@ -526,16 +612,16 @@
         ]
 
     for index in range(PLANES):
-        place = pl.ds((1 + FULL * index) * SUBLANES, FULL * SUBLANES)
-        start_fields[index, flat_rows(1, FULL), :] = low[place, :]
-        start_fields[index, flat_rows(2 * SLAB - HALO, FULL), :] = high[place, :]
+        low, high = received((1 + FULL * index) * SUBLANES, FULL)
+        start_fields[index, flat_rows(1, FULL), :] = low
+        start_fields[index, flat_rows(2 * SLAB - HALO, FULL), :] = high
         start_fields[index, flat_rows(HALO, 2), :] = whole[index, flat_rows(0, 2), :]
         start_fields[index, flat_rows(2 * SLAB - HALO - 2, 2), :] = whole[
             index, flat_rows(live - 2, 2), :
         ]
-    for row, end in ((0, low), (2 * SLAB - 1, high)):
+    for row, colour in zip((0, 2 * SLAB - 1), received(0, 1)):
         start_fields[0, flat_rows(row, 1), :] = jnp.zeros((SUBLANES, LANES), jnp.float32)
-        start_fields[10, flat_rows(row, 1), :] = 0.5 * end[pl.ds(0, SUBLANES), :]
+        start_fields[10, flat_rows(row, 1), :] = 0.5 * colour
 
     def place(target, index, source, at, first, size):
         for place, (row, local, count) in enumerate(spans(first, size)):
@@ -546,7 +632,7 @@
         if index >= MOVED:
             target, later, at = reds, reds_later, index - MOVED
         place(target, at, moved_rim, index, HALO + 1, 2)
-        place(later, at, moved_rim, MOVED + REDS + index, HALO + 3, 2)
+        place(later, at, moved_later_rim, index, HALO + 3, 2)
     for index in range(FIELDS):
         place(fields, index, fields_rim, index, HALO + 2, 2)
         place(final, index, final_rim, index, HALO + RIM, RIM)
@@ -567,7 +653,7 @@
 
     for index in range(FIELDS):
         for side, row in ((0, HALO), (1, SLAB)):
-            for tile in range(own_tiles):
+            for tile in range(OWN_TILES):
                 start = row * SUBLANES + 1 + tile
                 pieces[index, pl.ds(side * SUBLANES, SUBLANES), pl.ds(tile * LANES, LANES)] = final[
                     index, pl.ds(start, SUBLANES, stride=SUBLANES), :
@@ -591,13 +677,13 @@
         copy.wait()
 
 
-def run_outer(info, whole, low, high, rims, outs):
+def run_outer(info, whole, arrived, passed, rims, outs):
     flat = 2 * SLAB * SUBLANES
     flat_count = outs[0].shape[1]
     return pl.pallas_call(
         outer_kernel,
         out_shape=[jax.ShapeDtypeStruct(out.shape, jnp.float32) for out in outs],
-        in_specs=[SMEM] + [VMEM] * 6 + [ANY] * 4,
+        in_specs=[SMEM] + [VMEM] * 7 + [ANY] * 4,
         out_specs=[ANY] * 4,
         scratch_shapes=[
             pltpu.VMEM((PLANES, flat, LANES), jnp.float32),
@@ -612,33 +698,28 @@
             pltpu.VMEM((FIELDS, 2 * SUBLANES, flat_count), jnp.float32),
             pltpu.SemaphoreType.DMA((2, 4)),
         ],
-        input_output_aliases={7: 0, 8: 1, 9: 2, 10: 3},
+        input_output_aliases={8: 0, 9: 1, 10: 2, 11: 3},
         compiler_params=pltpu.CompilerParams(vmem_limit_bytes=32 * 1024 * 1024),
         name="outer",
-    )(info, whole, low, high, *rims, *outs)
+    )(info, whole, arrived, passed, *rims, *outs)
 
 
 def body(density, momentum, stress, red_density, solid, widths):
-    tiles_index = lax.axis_index("tiles")
     tiles_count = lax.axis_size("tiles")
-    chosen = lax.iota(jnp.int32, widths.shape[0]) == tiles_index
-    live_rows = jnp.sum(jnp.where(chosen, widths, 0)) * TILE
-    info = jnp.stack(
-        [
-            live_rows,
-            (tiles_index == 0).astype(jnp.int32),
-            (tiles_index == tiles_count - 1).astype(jnp.int32),
-            lax.axis_index("sub").astype(jnp.int32),
-        ]
-    )
     arrays = (density, momentum, stress, red_density, solid)
-    side = lax.ppermute(take_edge(arrays), "sub", [(0, 1), (1, 0)])
-    whole, low_end, high_end = take_ends(info, spread_rows(arrays), side)
-    ends = tiles_count - 1
-    low = lax.ppermute(high_end, "tiles", [(i, i + 1) for i in range(ends)])
-    high = lax.ppermute(low_end, "tiles", [(i + 1, i) for i in range(ends)])
-    results = run_inner(info, whole, arrays)
-    return tuple(run_outer(info, whole, low, high, results[4:], results[:4]))
+    info, spread, packet, mine = load_inputs(arrays, widths, tiles_count)
+    swap = [(0, 1), (1, 0)]
+    packet = lax.ppermute(packet, "sub", swap)
+    whole, ends = join_parts(info, spread, packet, mine)
+    route = [(2 * k, 2 * k + 2) for k in range(tiles_count - 1)]
+    route = route + [(2 * k + 3, 2 * k + 1) for k in range(tiles_count - 1)]
+    arrived = lax.ppermute(ends, ("tiles", "sub"), route)
+    fields, moved_rim, fields_rim = run_first(info, whole)
+    arrived, passing = turn_ends(info, arrived, fields_rim)
+    passed = lax.ppermute(passing, "sub", swap)
+    results = run_second(info, whole, fields, arrived, arrays)
+    rims = (moved_rim, fields_rim) + tuple(results[4:])
+    return tuple(run_outer(info, whole, arrived, passed, rims, results[:4]))
 
 
 def solution(mesh):

time: 29.7 us -> 33 us (1.11)
  the two profiles are of different devices: /device:TPU:19 before, /device:TPU:5 now
where the time goes in v3:
time: 33 us; the launch traced here: 32.7 us
  Pallas kernels  16.8 us (51%)
  starting transfers between devices  6.51 us (20%)
  local copies, waits for them, and re-layouts  5.56 us (17%)
  waiting for transfers between devices  3.16 us (10%)
  between operations  0.69 us (2%)
    pallas_call x1, Pallas kernels, run_second(): pl.pallas_call(second_kernel, out_shape=shapes, in_specs=[SMEM, VMEM, VME...  5.85 us
    unnamed x12, local copies, waits for them, and re-layouts  5.56 us
    pallas_call x1, Pallas kernels, run_first(): pl.pallas_call(first_kernel, out_shape=shapes, in_specs=[SMEM, VMEM], out...  4.89 us
    ppermute x1, starting transfers between devices, body(): passed = lax.ppermute(passing, 'sub', swap)  3.83 us
    pallas_call x1, Pallas kernels, run_outer(): pl.pallas_call(outer_kernel, out_shape=[jax.ShapeDtypeStruct(out.shape, j...  2.72 us
    ppermute x1, starting transfers between devices, body(): arrived = lax.ppermute(ends, ('tiles', 'sub'), route)  1.92 us
    pallas_call x1, Pallas kernels, load_inputs(): pl.pallas_call(functools.partial(load_kernel, tiles_count), out_shape=[ja...  1.9 us
    ppermute x1, waiting for transfers between devices, body(): arrived = lax.ppermute(ends, ('tiles', 'sub'), route)  1.73 us
  transfers between devices with their start and end apart: 3, of which 2 were waited for; matrix products, arithmetic and copies ran while one was open for 0% of the time, Pallas kernels for 33%

profile of v3, /device:TPU:5, one launch (start us, length us, event | category | flops | bytes accessed | tf_op | source)
XLA Modules:
  0.0 32.7 jit_solution(6298340401236749570)
XLA Ops:
  0.6 0.0 copy-start
  0.6 1.2 %copy-done = f32[6,48,768]{2,1,0:T(8,128)S(1)} copy-done((f32[6,48,768]{2,1,0:T(8,128)S(1)}, f32[6,48,768]{2,1,0:T(8,128)}, u32[]{:S(2)}) %copy-start) | copy-done | bytes 884760
  1.8 0.0 copy-start.1
  1.8 1.0 %copy-done.1 = f32[3,48,768]{2,1,0:T(8,128)S(1)} copy-done((f32[3,48,768]{2,1,0:T(8,128)S(1)}, f32[3,48,768]{2,1,0:T(8,128)}, u32[]{:S(2)}) %copy-start.1) | copy-done | bytes 442392
  2.8 0.0 copy-start.2
  2.8 0.9 %copy-done.2 = f32[48,768]{1,0:T(8,128)S(1)} copy-done((f32[48,768]{1,0:T(8,128)S(1)}, f32[48,768]{1,0:T(8,128)}, u32[]{:S(2)}) %copy-start.2) | copy-done | bytes 147480
  3.7 0.0 copy-start.3
  3.7 0.9 %copy-done.3 = f32[48,768]{1,0:T(8,128)S(1)} copy-done((f32[48,768]{1,0:T(8,128)S(1)}, f32[48,768]{1,0:T(8,128)}, u32[]{:S(2)}) %copy-start.3) | copy-done | bytes 147480
  4.6 0.0 copy-start.4
  4.6 0.9 %copy-done.4 = s32[48,768]{1,0:T(8,128)S(1)} copy-done((s32[48,768]{1,0:T(8,128)S(1)}, s32[48,768]{1,0:T(8,128)}, u32[]{:S(2)}) %copy-start.4) | copy-done | bytes 147480
  5.5 0.0 copy-start.5
  5.5 0.7 %copy-done.5 = s32[8]{0:T(128)S(1)} copy-done((s32[8]{0:T(128)S(1)}, s32[8]{0:T(128)}, u32[]{:S(2)}) %copy-start.5) | copy-done | bytes 56
  6.2 1.9 %load.1 = (s32[4]{0:T(128)S(1)}, f32[12,384,128]{2,1,0:T(8,128)S(1)}, f32[872,128]{1,0:T(8,128)S(1)}, f32[296,128]{1,0:T(8,128)S(1)}) custom-call(f32[48,768]{1,0:T(8,128)S(1)} %copy-done.2, f32[3,48,768]{2,1,0:T(8,128)S(1)} %copy-done.1, f32[6,48,768]{2,1,0:T(8,128)S(1)} %copy-done, f32[48,768]{1,0:T(8,128)S(1)} %copy-done.3, s32[48,768]{1,0:T(8,128)S(1)} %copy-done.4, ...), custom_call_target="tpu_custom_call" | custom-call | tf_op jit(solution)/shard_map/load/pallas_call | solution.py:401
  8.1 0.8 %collective-permute-start = (f32[872,128]{1,0:T(8,128)S(1)}, f32[872,128]{1,0:T(8,128)S(1)}, u32[]{:S(2)}, u32[]{:S(2)}) collective-permute-start(f32[872,128]{1,0:T(8,128)S(1)} %get-tuple-element.23), channel_id=1, source_target_pairs={{0,1},{1,0},{2,3},{3,2},{4,5},{5,4},{6,7},{7,6},{8,9},{9,8},{10,11... | collective-permute-start | bytes 1339400 | tf_op jit(solution)/shard_map/ppermute | solution.py:712
  8.9 1.4 %collective-permute-done.packet = f32[872,128]{1,0:T(8,128)S(1)} collective-permute-done((f32[872,128]{1,0:T(8,128)S(1)}, f32[872,128]{1,0:T(8,128)S(1)}, u32[]{:S(2)}, u32[]{:S(2)}) %collective-permute-start) | collective-permute-done | bytes 446496 | tf_op jit(solution)/shard_map/ppermute | solution.py:712
  10.3 0.8 %join.1 = (f32[12,384,128]{2,1,0:T(8,128)S(1)}, f32[592,128]{1,0:T(8,128)S(1)}) custom-call(s32[4]{0:T(128)S(1)} %get-tuple-element.21.info, f32[12,384,128]{2,1,0:T(8,128)S(1)} %get-tuple-element.22.spread, f32[872,128]{1,0:T(8,128)S(1)} %collective-permute-done.packet, f32[296,128]{1,0:T(8,128)S(1)} %get-tuple-element.24.mine), custom_call_target="tpu_custom_call" | custom-call | tf_op jit(solution)/shard_map/join/pallas_call | solution.py:439
  11.1 1.9 %collective-permute-start.1 = (f32[592,128]{1,0:T(8,128)S(1)}, f32[592,128]{1,0:T(8,128)S(1)}, u32[]{:S(2)}, u32[]{:S(2)}) collective-permute-start(f32[592,128]{1,0:T(8,128)S(1)} %get-tuple-element.26), channel_id=1, source_target_pairs={{0,2},{2,4},{4,6},{6,8},{8,10},{10,12},{12,14},{3,1},{5,3},{7,5},{... | collective-permute-start | bytes 909320 | tf_op jit(solution)/shard_map/ppermute | solution.py:716
  13.0 4.9 %first.1 = (f32[11,384,128]{2,1,0:T(8,128)S(1)}, f32[24,32,128]{2,1,0:T(8,128)S(1)}, f32[11,32,128]{2,1,0:T(8,128)S(1)}) custom-call(s32[4]{0:T(128)S(1)} %get-tuple-element.21.info, f32[12,384,128]{2,1,0:T(8,128)S(1)} %get-tuple-element.25.whole), custom_call_target="tpu_custom_call" | custom-call | flops 20000000 | bytes 8000000 | tf_op jit(solution)/shard_map/first/pallas_call | solution.py:533
  17.9 1.7 %collective-permute-done.1.ends = f32[592,128]{1,0:T(8,128)S(1)} collective-permute-done((f32[592,128]{1,0:T(8,128)S(1)}, f32[592,128]{1,0:T(8,128)S(1)}, u32[]{:S(2)}, u32[]{:S(2)}) %collective-permute-start.1) | collective-permute-done | bytes 303136 | tf_op jit(solution)/shard_map/ppermute | solution.py:716
  19.7 0.6 %turn.1 = (f32[296,128]{1,0:T(8,128)S(1)}, f32[296,128]{1,0:T(8,128)S(1)}) custom-call(s32[4]{0:T(128)S(1)} %get-tuple-element.21.info, f32[592,128]{1,0:T(8,128)S(1)} %collective-permute-done.1.ends, f32[11,32,128]{2,1,0:T(8,128)S(1)} %get-tuple-element.27.kept.fields_rim), custom_call_target="tpu_custom_call" | custom-call | tf_op jit(solution)/shard_map/turn/pallas_call | solution.py:581
  20.3 3.8 %collective-permute-start.2 = (f32[296,128]{1,0:T(8,128)S(1)}, f32[296,128]{1,0:T(8,128)S(1)}, u32[]{:S(2)}, u32[]{:S(2)}) collective-permute-start(f32[296,128]{1,0:T(8,128)S(1)} %get-tuple-element.29), channel_id=1, source_target_pairs={{0,1},{1,0},{2,3},{3,2},{4,5},{5,4},{6,7},{7,6},{8,9},{9,8},{10,11... | collective-permute-start | bytes 454664 | tf_op jit(solution)/shard_map/ppermute | solution.py:719
  24.1 5.8 %second.1 = (f32[48,768]{1,0:T(8,128)}, f32[3,48,768]{2,1,0:T(8,128)}, f32[6,48,768]{2,1,0:T(8,128)}, f32[48,768]{1,0:T(8,128)}, f32[24,32,128]{2,1,0:T(8,128)S(1)}, /*index=5*/f32[11,64,128]{2,1,0:T(8,128)S(1)}) custom-call(s32[4]{0:T(128)S(1)} %get-tuple-element.21.info, f32[12,384,128]{2,1,0:T(8,128)S(1)} %get-tuple-element.25.whole, ...), custom_call_target="tpu_custom_call" | custom-call | flops 20000000 | bytes 8000000 | tf_op jit(solution)/shard_map/second/pallas_call | solution.py:549
  30.0 0.0 collective-permute-done.2.passed
  30.0 2.7 %outer.1 = (f32[48,768]{1,0:T(8,128)}, f32[3,48,768]{2,1,0:T(8,128)}, f32[6,48,768]{2,1,0:T(8,128)}, f32[48,768]{1,0:T(8,128)}) custom-call(s32[4]{0:T(128)S(1)} %get-tuple-element.21.info, f32[12,384,128]{2,1,0:T(8,128)S(1)} %get-tuple-element.25.whole, ...), custom_call_target="tpu_custom_call", output_to_operand_aliasing={{0}: (8, {}), {1}: (9, {}), {2}: (10, {}), {3}: (11, {})} | custom-call | tf_op jit(solution)/shard_map/outer/pallas_call | solution.py:683
Async XLA Ops:
  0.6 1.2 %copy-start = (f32[6,48,768]{2,1,0:T(8,128)S(1)}, f32[6,48,768]{2,1,0:T(8,128)}, u32[]{:S(2)}) copy-start(f32[6,48,768]{2,1,0:T(8,128)} %stress.1) | copy-start | bytes 2654212
  1.8 1.0 %copy-start.1 = (f32[3,48,768]{2,1,0:T(8,128)S(1)}, f32[3,48,768]{2,1,0:T(8,128)}, u32[]{:S(2)}) copy-start(f32[3,48,768]{2,1,0:T(8,128)} %momentum.1) | copy-start | bytes 1327108
  2.8 0.9 %copy-start.2 = (f32[48,768]{1,0:T(8,128)S(1)}, f32[48,768]{1,0:T(8,128)}, u32[]{:S(2)}) copy-start(f32[48,768]{1,0:T(8,128)} %density.1) | copy-start | bytes 442372
  3.7 0.9 %copy-start.3 = (f32[48,768]{1,0:T(8,128)S(1)}, f32[48,768]{1,0:T(8,128)}, u32[]{:S(2)}) copy-start(f32[48,768]{1,0:T(8,128)} %red.1) | copy-start | bytes 442372
  4.6 0.9 %copy-start.4 = (s32[48,768]{1,0:T(8,128)S(1)}, s32[48,768]{1,0:T(8,128)}, u32[]{:S(2)}) copy-start(s32[48,768]{1,0:T(8,128)} %solid.1) | copy-start | bytes 442372
  5.5 0.7 %copy-start.5 = (s32[8]{0:T(128)S(1)}, s32[8]{0:T(128)}, u32[]{:S(2)}) copy-start(s32[8]{0:T(128)} %widths.1) | copy-start | bytes 100
  8.1 2.2 %collective-permute-start = (f32[872,128]{1,0:T(8,128)S(1)}, f32[872,128]{1,0:T(8,128)S(1)}, u32[]{:S(2)}, u32[]{:S(2)}) collective-permute-start(f32[872,128]{1,0:T(8,128)S(1)} %get-tuple-element.23), channel_id=1, source_target_pairs={{0,1},{1,0},{2,3},{3,2},{4,5},{5,4},{6,7},{7,6},{8,9},{9,8},{10,11... | collective-permute-start | bytes 1339400 | tf_op jit(solution)/shard_map/ppermute | solution.py:712
  11.1 8.6 %collective-permute-start.1 = (f32[592,128]{1,0:T(8,128)S(1)}, f32[592,128]{1,0:T(8,128)S(1)}, u32[]{:S(2)}, u32[]{:S(2)}) collective-permute-start(f32[592,128]{1,0:T(8,128)S(1)} %get-tuple-element.26), channel_id=1, source_target_pairs={{0,2},{2,4},{4,6},{6,8},{8,10},{10,12},{12,14},{3,1},{5,3},{7,5},{... | collective-permute-start | bytes 909320 | tf_op jit(solution)/shard_map/ppermute | solution.py:716
  20.3 9.7 %collective-permute-start.2 = (f32[296,128]{1,0:T(8,128)S(1)}, f32[296,128]{1,0:T(8,128)S(1)}, u32[]{:S(2)}, u32[]{:S(2)}) collective-permute-start(f32[296,128]{1,0:T(8,128)S(1)} %get-tuple-element.29), channel_id=1, source_target_pairs={{0,1},{1,0},{2,3},{3,2},{4,5},{5,4},{6,7},{7,6},{8,9},{9,8},{10,11... | collective-permute-start | bytes 454664 | tf_op jit(solution)/shard_map/ppermute | solution.py:719

commit v4 on v2

--- a/solution.py
+++ b/solution.py
@@ -635,8 +635,15 @@
     side = lax.ppermute(take_edge(arrays), "sub", [(0, 1), (1, 0)])
     whole, low_end, high_end = take_ends(info, spread_rows(arrays), side)
     ends = tiles_count - 1
-    low = lax.ppermute(high_end, "tiles", [(i, i + 1) for i in range(ends)])
-    high = lax.ppermute(low_end, "tiles", [(i + 1, i) for i in range(ends)])
+    odd = tiles_index % 2 == 1
+    even_groups = [[2 * k, 2 * k + 1] for k in range(tiles_count // 2)]
+    odd_groups = [[2 * k + 1, (2 * k + 2) % tiles_count] for k in range(tiles_count // 2)]
+    pair = lax.all_gather(jnp.where(odd, low_end, high_end), "tiles", axis_index_groups=even_groups)
+    other = lax.all_gather(jnp.where(odd, high_end, low_end), "tiles", axis_index_groups=odd_groups)
+    low = jnp.where(odd, pair[0], other[0])
+    high = jnp.where(odd, other[1], pair[1])
+    low = jnp.where(tiles_index == 0, 0.0, low)
+    high = jnp.where(tiles_index == tiles_count - 1, 0.0, high)
     results = run_inner(info, whole, arrays)
     return tuple(run_outer(info, whole, low, high, results[4:], results[:4]))
 

time: 29.7 us -> 39.6 us (1.33)
  the two profiles are of different devices: /device:TPU:19 before, /device:TPU:0 now
where the time goes in v4:
time: 39.6 us; the launch traced here: 40.1 us
  blocking collectives  17 us (43%)
  Pallas kernels  16.6 us (42%)
  local copies, waits for them, and re-layouts  3.75 us (9%)
  between operations  1.39 us (4%)
  other arithmetic  0.87 us (2%)
  starting transfers between devices  0.52 us (1%)
    pallas_call x1, Pallas kernels, run_inner(): pl.pallas_call(inner_kernel, out_shape=shapes, in_specs=[SMEM, VMEM], out...  11 us
    all_gather x1, blocking collectives, body(): lax.all_gather(jnp.where(odd, high_end, low_end), 'tiles', axis_index_gro...  9.23 us
    all_gather x1, blocking collectives, body(): lax.all_gather(jnp.where(odd, low_end, high_end), 'tiles', axis_index_gro...  7.78 us
    unnamed x12, local copies, waits for them, and re-layouts  3.75 us
    pallas_call x1, Pallas kernels, run_outer(): pl.pallas_call(outer_kernel, out_shape=[jax.ShapeDtypeStruct(out.shape, j...  2.73 us
    pallas_call x1, Pallas kernels, take_edge(): pl.pallas_call(edge_kernel, out_shape=jax.ShapeDtypeStruct((PLANES, row_c...  1.81 us
    pallas_call x1, Pallas kernels, take_ends(): pl.pallas_call(ends_kernel, out_shape=[jax.ShapeDtypeStruct(spread.shape,...  0.81 us
  transfers between devices with their start and end apart: 1, of which 0 were waited for; matrix products, arithmetic and copies ran while one was open for 2% of the time, Pallas kernels for 1%

profile of v4, /device:TPU:0, one launch (start us, length us, event | category | flops | bytes accessed | tf_op | source)
XLA Modules:
  0.0 40.1 jit_solution(6988430658013483526)
XLA Ops:
  0.6 0.0 copy-start
  0.6 1.8 %edge.1 = f32[12,48,128]{2,1,0:T(8,128)} custom-call(f32[48,768]{1,0:T(8,128)} %density.3, f32[3,48,768]{2,1,0:T(8,128)} %momentum.3, f32[6,48,768]{2,1,0:T(8,128)} %stress.3, f32[48,768]{1,0:T(8,128)} %red.3, s32[48,768]{1,0:T(8,128)} %solid.3), custom_call_target="tpu_custom_call" | custom-call | tf_op jit(solution)/shard_map/edge/pallas_call | solution.py:357
  2.5 0.0 copy-start.5
  2.5 0.5 %collective-permute-start = (f32[12,48,128]{2,1,0:T(8,128)}, f32[12,48,128]{2,1,0:T(8,128)S(1)}, u32[]{:S(2)}, u32[]{:S(2)}) collective-permute-start(f32[12,48,128]{2,1,0:T(8,128)} %edge.1), channel_id=1, source_target_pairs={{0,1},{1,0},{2,3},{3,2},{4,5},{5,4},{6,7},{7,6},{8,9},{9,8},{10,11... | collective-permute-start | bytes 884744 | tf_op jit(solution)/shard_map/ppermute | solution.py:635
  3.0 0.0 copy-done
  3.0 0.0 copy-start.1
  3.0 1.0 %copy-done.1 = f32[3,48,768]{2,1,0:T(8,128)S(1)} copy-done((f32[3,48,768]{2,1,0:T(8,128)S(1)}, f32[3,48,768]{2,1,0:T(8,128)}, u32[]{:S(2)}) %copy-start.1) | copy-done | bytes 442392
  4.0 0.0 copy-start.2
  4.0 0.9 %copy-done.2 = f32[48,768]{1,0:T(8,128)S(1)} copy-done((f32[48,768]{1,0:T(8,128)S(1)}, f32[48,768]{1,0:T(8,128)}, u32[]{:S(2)}) %copy-start.2) | copy-done | bytes 147480
  4.9 0.0 copy-start.3
  4.9 0.9 %copy-done.3 = f32[48,768]{1,0:T(8,128)S(1)} copy-done((f32[48,768]{1,0:T(8,128)S(1)}, f32[48,768]{1,0:T(8,128)}, u32[]{:S(2)}) %copy-start.3) | copy-done | bytes 147480
  5.8 0.0 copy-start.4
  5.8 0.9 %copy-done.4 = s32[48,768]{1,0:T(8,128)S(1)} copy-done((s32[48,768]{1,0:T(8,128)S(1)}, s32[48,768]{1,0:T(8,128)}, u32[]{:S(2)}) %copy-start.4) | copy-done | bytes 147480
  6.7 0.3 spread.1
  7.1 0.0 copy-done.5
  7.1 0.7 %fusion.2 = s32[]{:T(128)} fusion(s32[8]{0:T(128)S(1)} %copy-done.5, s32[]{:T(128)S(6)} %axis_index.23), kind=kLoop, calls=%fused_computation.7 | loop fusion | flops 23 | bytes 40 | tf_op jit(solution)/shard_map/reduce_sum | solution.py:625
  8.5 0.1 pad_add_fusion.info
  8.5 0.0 collective-permute-done.side
  8.5 0.8 %ends.1 = (f32[12,384,128]{2,1,0:T(8,128)S(1)}, f32[296,128]{1,0:T(8,128)S(1)}, f32[296,128]{1,0:T(8,128)S(1)}) custom-call(s32[4]{0:T(128)S(1)} %pad_add_fusion.info, f32[12,384,128]{2,1,0:T(8,128)S(1)} %spread.1, f32[12,48,128]{2,1,0:T(8,128)S(1)} %collective-permute-done.side), custom_call_target="tpu_custom_call" | custom-call | tf_op jit(solution)/shard_map/ends/pallas_call | solution.py:414
  9.4 7.8 %all-gather = f32[592,128]{1,0:T(8,128)S(1)} all-gather(f32[296,128]{1,0:T(8,128)S(1)} %get-tuple-element.26), channel_id=2, replica_groups={{0,2},{4,6},{8,10},{12,14},{1,3},{5,7},{9,11},{13,15},{16,18},{20,22},{..., dimensions={0}, use_global_device_ids=true | all-gather | bytes 454656 | tf_op jit(solution)/shard_map/all_gather | solution.py:641
  17.2 9.2 %all-gather.1 = f32[592,128]{1,0:T(8,128)S(1)} all-gather(f32[296,128]{1,0:T(8,128)S(1)} %get-tuple-element.27), channel_id=3, replica_groups={{2,4},{6,8},{10,12},{14,0},{3,5},{7,9},{11,13},{15,1},{18,20},{22,24},{..., dimensions={0}, use_global_device_ids=true | all-gather | bytes 454656 | tf_op jit(solution)/shard_map/all_gather | solution.py:642
  26.4 11.0 %inner.1 = (f32[48,768]{1,0:T(8,128)}, f32[3,48,768]{2,1,0:T(8,128)}, f32[6,48,768]{2,1,0:T(8,128)}, f32[48,768]{1,0:T(8,128)}, f32[48,32,128]{2,1,0:T(8,128)S(1...) custom-call(s32[4]{0:T(128)S(1)} %pad_add_fusion.info, f32[12,384,128]{2,1,0:T(8,128)S(1)} %get-tuple-element.14.whole), custom_call_target="tpu_custom_call" | custom-call | flops 40000000 | bytes 8000000 | tf_op jit(solution)/shard_map/inner/pallas_call | solution.py:488
  37.4 2.7 %outer.1 = (f32[48,768]{1,0:T(8,128)}, f32[3,48,768]{2,1,0:T(8,128)}, f32[6,48,768]{2,1,0:T(8,128)}, f32[48,768]{1,0:T(8,128)}) custom-call(s32[4]{0:T(128)S(1)} %pad_add_fusion.info, f32[12,384,128]{2,1,0:T(8,128)S(1)} %get-tuple-element.14.whole, ...), custom_call_target="tpu_custom_call", output_to_operand_aliasing={{0}: (7, {}), {1}: (8, {}), {2}: (9, {}), {3}: (10, {})} | custom-call | tf_op jit(solution)/shard_map/outer/pallas_call | solution.py:597
  (2 shorter events, 0.1 us)
Async XLA Ops:
  0.6 2.4 %copy-start = (f32[6,48,768]{2,1,0:T(8,128)S(1)}, f32[6,48,768]{2,1,0:T(8,128)}, u32[]{:S(2)}) copy-start(f32[6,48,768]{2,1,0:T(8,128)} %stress.3) | copy-start | bytes 2654212
  2.5 4.6 %copy-start.5 = (s32[8]{0:T(128)S(1)}, s32[8]{0:T(128)}, u32[]{:S(2)}) copy-start(s32[8]{0:T(128)} %param.11) | copy-start | bytes 100
  2.5 6.1 %collective-permute-start = (f32[12,48,128]{2,1,0:T(8,128)}, f32[12,48,128]{2,1,0:T(8,128)S(1)}, u32[]{:S(2)}, u32[]{:S(2)}) collective-permute-start(f32[12,48,128]{2,1,0:T(8,128)} %edge.1), channel_id=1, source_target_pairs={{0,1},{1,0},{2,3},{3,2},{4,5},{5,4},{6,7},{7,6},{8,9},{9,8},{10,11... | collective-permute-start | bytes 884744 | tf_op jit(solution)/shard_map/ppermute | solution.py:635
  3.0 1.0 %copy-start.1 = (f32[3,48,768]{2,1,0:T(8,128)S(1)}, f32[3,48,768]{2,1,0:T(8,128)}, u32[]{:S(2)}) copy-start(f32[3,48,768]{2,1,0:T(8,128)} %momentum.3) | copy-start | bytes 1327108
  4.0 0.9 %copy-start.2 = (f32[48,768]{1,0:T(8,128)S(1)}, f32[48,768]{1,0:T(8,128)}, u32[]{:S(2)}) copy-start(f32[48,768]{1,0:T(8,128)} %density.3) | copy-start | bytes 442372
  4.9 0.9 %copy-start.3 = (f32[48,768]{1,0:T(8,128)S(1)}, f32[48,768]{1,0:T(8,128)}, u32[]{:S(2)}) copy-start(f32[48,768]{1,0:T(8,128)} %red.3) | copy-start | bytes 442372
  5.8 0.9 %copy-start.4 = (s32[48,768]{1,0:T(8,128)S(1)}, s32[48,768]{1,0:T(8,128)}, u32[]{:S(2)}) copy-start(s32[48,768]{1,0:T(8,128)} %solid.3) | copy-start | bytes 442372
